TPU v7x, 256 devices: a whole 4x4x8 slice. The times are simulated.
256 devices in a mesh: ctx: 8 (over z), head: 32 (over x, y, core).
Axes of the slice: x: 4, y: 4, z: 8, core: 2. Of those that a mesh axis runs over, the one named last changes fastest.
Arguments:
- queries: bfloat16 [4096, 64, 128], P(('ctx', 'head')), may hold values from -8 to 8, as said below
- keys: bfloat16 [8, 64, 8, 128, 128], P(None, 'head', 'ctx'), may hold values from -4 to 4, as said below
- values: bfloat16 [8, 64, 8, 128, 128], P(None, 'head', 'ctx'), may hold values from -6 to 6
- outputs: bfloat16 [4096, 64, 128], P(('ctx', 'head')), may hold values from -1 to 1
- grad_out: bfloat16 [4096, 64, 128], P(('ctx', 'head')), may hold values from -40 to 40
- block_ids: int32 [32, 8, 48], replicated, may hold values from 0 to 511, as said below
- block_counts: int32 [32, 8], replicated, may hold values from 1 to 48, as said below
Outputs:
- grad_queries: bfloat16 [4096, 64, 128], P(('ctx', 'head'))
- grad_keys: bfloat16 [8, 64, 8, 128, 128], P(None, 'head', 'ctx')
- grad_values: bfloat16 [8, 64, 8, 128, 128], P(None, 'head', 'ctx')
Inputs may be any that keep to these rules, and one draw needn't show every extreme that they name: queries are of order one. keys are of order one. block_ids[i, h, 0] = 480 + i, the key block that holds query block i's own positions, and slots from block_counts[i, h] on repeat it; the other live slots hold distinct key blocks before the query slab. Key block g belongs to context group g % 8. The live lists of the query blocks of one context group for one key head name at most 7 distinct blocks of any one group, and in every draw some group and key head name exactly 7 from every group. `block_counts`: some context group has all its lists full for some key head.
All inputs are finite; a program needn't handle non-finite values.
Results may differ from a plain program's by a relative error of at most 0.0049.
Values may be sent and summed in bfloat16 or wider, within the bound.
A program may use at most 128 MiB of HBM per device.

v0:
```python
import jax
import jax.numpy as jnp
from jax import lax
from jax.sharding import PartitionSpec as P

neg_fill = -1e30
slot_step = 8


def masked_scores(query_part, key_part, allowed, scaling):
    score = (
        jnp.einsum("kqhd,ksd->khqs", query_part, key_part, preferred_element_type=jnp.float32)
        * scaling
    )
    return jnp.where(allowed[:, None], score, neg_fill)


def update_stats(running, score, allowed):
    top_old, mass_old = running
    top_new = jnp.maximum(top_old, jnp.max(score, axis=-1))
    weight = jnp.where(allowed[:, None], jnp.exp(score - top_new[..., None]), 0.0)
    return (top_new, mass_old * jnp.exp(top_old - top_new) + jnp.sum(weight, axis=-1))


def grad_terms(query_part, grad_part, delta_part, key_part, value_part, allowed, stats, scaling):
    top_fin, mass_fin = stats
    score = masked_scores(query_part, key_part, allowed, scaling)
    prob = (
        jnp.where(allowed[:, None], jnp.exp(score - top_fin[..., None]), 0.0) / mass_fin[..., None]
    )
    prob_low = prob.astype(jnp.bfloat16)
    dprob = jnp.einsum("kqhd,ksd->khqs", grad_part, value_part, preferred_element_type=jnp.float32)
    dscore = (prob * (dprob - delta_part[..., None])).astype(jnp.bfloat16)
    grad_q = (
        jnp.einsum("khqs,ksd->kqhd", dscore, key_part, preferred_element_type=jnp.float32) * scaling
    )
    grad_k = (
        jnp.einsum("khqs,kqhd->ksd", dscore, query_part, preferred_element_type=jnp.float32)
        * scaling
    )
    grad_v = jnp.einsum("khqs,kqhd->ksd", prob_low, grad_part, preferred_element_type=jnp.float32)
    return (grad_q, grad_k, grad_v)


def allowed_keys(key_block_ids, usable, query_block_ids, diag_base, blk_len):
    offsets = jnp.arange(blk_len, dtype=jnp.int32)
    key_pos = (key_block_ids[:, :, None] * blk_len + offsets).reshape(key_block_ids.shape[0], -1)
    ok_slot = jnp.repeat(usable, blk_len, axis=1)
    query_pos = (diag_base + query_block_ids)[:, None] * blk_len + offsets[None, :]
    return ok_slot[:, None, :] & (key_pos[:, None, :] <= query_pos[:, :, None])


def body(queries, keys, values, outputs, grad_out, block_ids, block_counts):
    ctx_count = lax.axis_size("ctx")
    head_count = lax.axis_size("head")
    group_id = lax.axis_index("ctx")
    member = lax.axis_index("head")
    kv_count = keys.shape[0]
    per_dev = keys.shape[1]
    blk_len = keys.shape[3]
    head_dim = keys.shape[4]
    heads_all = queries.shape[1]
    head_share = heads_all // head_count
    repeats = head_count // kv_count
    kv_head = member // repeats
    query_blocks = block_ids.shape[0]
    retained = block_ids.shape[2]
    per_group = per_dev * head_count
    key_blocks = per_group * ctx_count
    own_blocks = query_blocks // ctx_count
    capacity = (retained + own_blocks + ctx_count - 2) // ctx_count
    diag_base = key_blocks - query_blocks
    scaling = head_dim ** (-0.5)
    query_loc, grad_loc, out_loc = (
        lax.all_to_all(queries, "head", split_axis=1, concat_axis=0, tiled=True),
        lax.all_to_all(grad_out, "head", split_axis=1, concat_axis=0, tiled=True),
        lax.all_to_all(outputs, "head", split_axis=1, concat_axis=0, tiled=True),
    )
    delta = jnp.sum(grad_loc.astype(jnp.float32) * out_loc.astype(jnp.float32), axis=2)
    key_send = jnp.repeat(keys[:, :, 0], repeats, axis=0)
    value_send = jnp.repeat(values[:, :, 0], repeats, axis=0)
    key_held, value_held = (
        lax.all_to_all(key_send, "head", split_axis=0, concat_axis=1, tiled=True),
        lax.all_to_all(value_send, "head", split_axis=0, concat_axis=1, tiled=True),
    )
    key_held = key_held[0]
    value_held = value_held[0]
    block_list = lax.dynamic_index_in_dim(block_ids, kv_head, 1, keepdims=False)
    count_list = lax.dynamic_index_in_dim(block_counts, kv_head, 1, keepdims=False)
    usable = jnp.arange(retained, dtype=jnp.int32)[None, :] < count_list[:, None]
    source = block_list % ctx_count
    local_id = block_list // ctx_count
    stat_shape = (own_blocks, head_share, blk_len)
    zero_rows = jnp.zeros((per_group, blk_len, head_dim), jnp.float32)
    query_part_all = query_loc.reshape(own_blocks, blk_len, head_share, head_dim)
    grad_part_all = grad_loc.reshape(own_blocks, blk_len, head_share, head_dim)
    delta_part_all = jnp.transpose(delta.reshape(own_blocks, blk_len, head_share), (0, 2, 1))
    total_ids = ctx_count * per_group
    flat_id = source * per_group + local_id
    hits = (flat_id[:, :, None] == jnp.arange(total_ids, dtype=jnp.int32)) & usable[:, :, None]
    used = jnp.any(hits.reshape(ctx_count, own_blocks * retained, total_ids), axis=1)
    used = used.reshape(ctx_count, ctx_count, per_group)
    position = jnp.cumsum(used.astype(jnp.int32), axis=2) - 1
    mine = lax.dynamic_index_in_dim(used, group_id, 1, keepdims=False)
    mine_pos = lax.dynamic_index_in_dim(position, group_id, 1, keepdims=False)
    matches = mine[:, :, None] & (mine_pos[:, :, None] == jnp.arange(capacity, dtype=jnp.int32))
    send_ids = jnp.sum(
        jnp.where(matches, jnp.arange(per_group, dtype=jnp.int32)[None, :, None], 0), axis=1
    )
    key_got, value_got = (
        lax.all_to_all(key_held[send_ids], "ctx", split_axis=0, concat_axis=0, tiled=True),
        lax.all_to_all(value_held[send_ids], "ctx", split_axis=0, concat_axis=0, tiled=True),
    )
    key_got = key_got.reshape(ctx_count * capacity, blk_len, head_dim)
    value_got = value_got.reshape(ctx_count * capacity, blk_len, head_dim)
    own_pos = lax.dynamic_index_in_dim(position, group_id, 0, keepdims=False)
    lookup = (jnp.arange(ctx_count, dtype=jnp.int32)[:, None] * capacity + own_pos).reshape(-1)
    own_flat = lax.dynamic_slice_in_dim(flat_id, group_id * own_blocks, own_blocks, 0)
    slot_index = jnp.sum(
        jnp.where(own_flat[:, :, None] == jnp.arange(total_ids, dtype=jnp.int32), lookup, 0), axis=2
    )
    slot_index = jnp.clip(slot_index, 0, ctx_count * capacity - 1)
    own_list = lax.dynamic_slice_in_dim(block_list, group_id * own_blocks, own_blocks, 0)
    own_usable = lax.dynamic_slice_in_dim(usable, group_id * own_blocks, own_blocks, 0)
    own_counts = lax.dynamic_slice_in_dim(count_list, group_id * own_blocks, own_blocks, 0)
    own_query_ids = group_id * own_blocks + jnp.arange(own_blocks, dtype=jnp.int32)
    rounds = (jnp.max(own_counts) + slot_step - 1) // slot_step

    def turn_inputs(turn):
        begin = turn * slot_step
        slots = lax.dynamic_slice_in_dim(slot_index, begin, slot_step, 1)
        allowed = allowed_keys(
            lax.dynamic_slice_in_dim(own_list, begin, slot_step, 1),
            lax.dynamic_slice_in_dim(own_usable, begin, slot_step, 1),
            own_query_ids,
            diag_base,
            blk_len,
        )
        key_part = key_got[slots].reshape(own_blocks, slot_step * blk_len, head_dim)
        value_part = value_got[slots].reshape(own_blocks, slot_step * blk_len, head_dim)
        return (slots, allowed, key_part, value_part)

    def stats_turn(turn, running):
        slots, allowed, key_part, value_part = turn_inputs(turn)
        score = masked_scores(query_part_all, key_part, allowed, scaling)
        return update_stats(running, score, allowed)

    stats = lax.fori_loop(
        0,
        rounds,
        stats_turn,
        (jnp.full(stat_shape, neg_fill, jnp.float32), jnp.zeros(stat_shape, jnp.float32)),
    )

    def grad_turn(turn, carried):
        grad_q, grad_kf, grad_vf = carried
        slots, allowed, key_part, value_part = turn_inputs(turn)
        part_q, part_k, part_v = grad_terms(
            query_part_all,
            grad_part_all,
            delta_part_all,
            key_part,
            value_part,
            allowed,
            stats,
            scaling,
        )
        flat_slots = slots.reshape(-1)
        grad_kf = grad_kf.at[flat_slots].add(
            part_k.reshape(own_blocks * slot_step, blk_len, head_dim)
        )
        grad_vf = grad_vf.at[flat_slots].add(
            part_v.reshape(own_blocks * slot_step, blk_len, head_dim)
        )
        return (grad_q + part_q, grad_kf, grad_vf)

    fetched_zero = jnp.zeros((ctx_count * capacity, blk_len, head_dim), jnp.float32)
    grad_q, grad_kf, grad_vf = lax.fori_loop(
        0,
        rounds,
        grad_turn,
        (
            jnp.zeros((own_blocks, blk_len, head_share, head_dim), jnp.float32),
            fetched_zero,
            fetched_zero,
        ),
    )
    back_k, back_v = (
        lax.all_to_all(
            grad_kf.reshape(ctx_count, capacity, blk_len, head_dim),
            "ctx",
            split_axis=0,
            concat_axis=0,
            tiled=True,
        ),
        lax.all_to_all(
            grad_vf.reshape(ctx_count, capacity, blk_len, head_dim),
            "ctx",
            split_axis=0,
            concat_axis=0,
            tiled=True,
        ),
    )
    flat_send = send_ids.reshape(-1)
    grad_k_held = zero_rows.at[flat_send].add(back_k.reshape(-1, blk_len, head_dim))
    grad_v_held = zero_rows.at[flat_send].add(back_v.reshape(-1, blk_len, head_dim))
    owner_k, owner_v = (
        lax.all_to_all(
            grad_k_held.reshape(head_count, per_dev, blk_len, head_dim),
            "head",
            split_axis=0,
            concat_axis=0,
            tiled=True,
        ),
        lax.all_to_all(
            grad_v_held.reshape(head_count, per_dev, blk_len, head_dim),
            "head",
            split_axis=0,
            concat_axis=0,
            tiled=True,
        ),
    )
    grad_keys = jnp.sum(owner_k.reshape(kv_count, repeats, per_dev, blk_len, head_dim), axis=1)[
        :, :, None
    ].astype(jnp.bfloat16)
    grad_values = jnp.sum(owner_v.reshape(kv_count, repeats, per_dev, blk_len, head_dim), axis=1)[
        :, :, None
    ].astype(jnp.bfloat16)
    grad_low = grad_q.reshape(own_blocks * blk_len, head_share, head_dim).astype(jnp.bfloat16)
    grad_queries = lax.all_to_all(grad_low, "head", split_axis=0, concat_axis=1, tiled=True)
    return (grad_queries, grad_keys, grad_values)


def solution(mesh):
    placed = (
        P(("ctx", "head"), None, None),
        P(None, "head", "ctx", None, None),
        P(None, "head", "ctx", None, None),
        P(("ctx", "head"), None, None),
        P(("ctx", "head"), None, None),
        P(),
        P(),
    )
    return jax.shard_map(
        body,
        mesh=mesh,
        in_specs=placed,
        out_specs=(
            P(("ctx", "head"), None, None),
            P(None, "head", "ctx", None, None),
            P(None, "head", "ctx", None, None),
        ),
        check_vma=False,
    )
```

profile of v0, /device:TPU:1, one launch (start us, length us, event | category | flops | bytes accessed | tf_op | source)
XLA Modules:
  0.0 695.4 jit_solution(6500009298824282076)
XLA Ops:
  0.6 1.8 copy.54
  2.5 8.6 %all-to-all-start.2 = ((bf16[16,64,128]{2,0,1:T(8,128)(2,1)}), bf16[16,64,128]{2,0,1:T(8,128)(2,1)S(1)}, u32[]{:S(2)}, u32[]{:S(2)}) async-start(bf16[16,64,128]{2,0,1:T(8,128)(2,1)} %copy.54), calls=%async_computation.2 | async-start | bytes 524288 | tf_op jit(solution)/shard_map/all_to_all | solution.py:75
  11.1 1.8 copy.59
  12.9 7.2 %all-to-all-done.2 = bf16[16,64,128]{2,0,1:T(8,128)(2,1)S(1)} async-done(((bf16[16,64,128]{2,0,1:T(8,128)(2,1)}), bf16[16,64,128]{2,0,1:T(8,128)(2,1)S(1)}, u32[]{:S(2)}, u32[]{:S(2)}) %all-to-all-start.2) | async-done | bytes 262176 | tf_op jit(solution)/shard_map/all_to_all | solution.py:75
  20.0 3.7 all-to-all-start.6
  24.9 8.0 %all-to-all-done.6 = bf16[16,64,128]{2,0,1:T(8,128)(2,1)S(1)} async-done(((bf16[16,64,128]{2,0,1:T(8,128)(2,1)}), bf16[16,64,128]{2,0,1:T(8,128)(2,1)S(1)}, u32[]{:S(2)}, u32[]{:S(2)}) %all-to-all-start.6) | async-done | bytes 262176 | tf_op jit(solution)/shard_map/all_to_all | solution.py:77
  32.9 12.4 %all_to_all.105 = bf16[16,64,128]{2,0,1:T(8,128)(2,1)S(1)} all-to-all(bf16[16,64,128]{2,0,1:T(8,128)(2,1)S(1)} %copy.57), channel_id=1, replica_groups=mesh['ctx'=8,'head'=32] {'head'}, dimensions={1} | all-to-all | bytes 524288 | tf_op jit(solution)/shard_map/all_to_all | solution.py:76
  45.3 1.5 broadcast_in_dim.128
  46.8 31.8 %all_to_all.106 = bf16[32,2,128,128]{3,2,1,0:T(8,128)(2,1)} all-to-all(bf16[32,2,128,128]{3,2,1,0:T(8,128)(2,1)S(1)} %bitcast.247), channel_id=1, replica_groups=mesh['ctx'=8,'head'=32] {'head'}, dimensions={0} | all-to-all | bytes 4194304 | tf_op jit(solution)/shard_map/all_to_all | solution.py:83
  78.6 1.8 broadcast_in_dim.133
  80.4 3.9 all-to-all-start.3
  85.9 1.6 fusion.40
  88.4 1.8 reduce_window_sum.11
  90.6 3.7 gather_fusion.3
  94.3 18.4 %all-to-all-done.3 = bf16[32,2,128,128]{3,2,1,0:T(8,128)(2,1)S(1)} async-done(((bf16[32,2,128,128]{3,2,1,0:T(8,128)(2,1)}), bf16[32,2,128,128]{3,2,1,0:T(8,128)(2,1)S(1)}, u32[]{:S(2)}, u32[]{:S(2)}) %all-to-all-start.3) | async-done | bytes 2097184 | tf_op jit(solution)/shard_map/all_to_all | solution.py:84
  112.7 8.2 %all-to-all-start.1 = ((bf16[8,7,128,128]{3,2,1,0:T(8,128)(2,1)}), bf16[8,7,128,128]{3,2,1,0:T(8,128)(2,1)}, u32[]{:S(2)}, u32[]{:S(2)}) async-start(bf16[8,7,128,128]{3,2,1,0:T(8,128)(2,1)} %bitcast.250), calls=%async_computation.1 | async-start | bytes 3670016 | tf_op jit(solution)/shard_map/all_to_all | solution.py:111
  124.8 2.1 gather_fusion.4
  126.9 40.1 %all-to-all-done.1 = bf16[8,7,128,128]{3,2,1,0:T(8,128)(2,1)} async-done(((bf16[8,7,128,128]{3,2,1,0:T(8,128)(2,1)}), bf16[8,7,128,128]{3,2,1,0:T(8,128)(2,1)}, u32[]{:S(2)}, u32[]{:S(2)}) %all-to-all-start.1) | async-done | bytes 1835040 | tf_op jit(solution)/shard_map/all_to_all | solution.py:111
  167.0 4.3 all-to-all-start.4
  171.3 18.3 %while.28 = (s32[]{:T(128)}, f32[4,2,128]{2,1,0:T(2,128)S(1)}, f32[4,2,128]{2,1,0:T(2,128)S(1)}, s32[]{:T(128)}, pred[4,48]{1,0:T(4,128)(4,1)S(1)}, /*index=5*/s...) while((s32[]{:T(128)}, f32[4,2,128]{2,1,0:T(2,128)S(1)}, ...), condition=%wide.region_8.9_spmd.clone, body=%wide.region_5.8_spmd.clone.sunk | while | flops 277880480 | bytes 13522367 | solution.py:148
  171.8 1.4 compare_and_fusion.4
  173.3 2.2 gather_fusion
  178.0 1.4 compare_and_fusion.4
  179.4 2.2 gather_fusion
  185.5 2.2 gather_fusion
  189.7 24.8 %all-to-all-done.4 = bf16[8,7,128,128]{3,2,1,0:T(8,128)(2,1)} async-done(((bf16[8,7,128,128]{3,2,1,0:T(8,128)(2,1)}), bf16[8,7,128,128]{3,2,1,0:T(8,128)(2,1)}, u32[]{:S(2)}, u32[]{:S(2)}) %all-to-all-start.4) | async-done | bytes 1835040 | tf_op jit(solution)/shard_map/all_to_all | solution.py:112
  214.5 2.3 broadcast_in_dim.125.clone
  216.8 2.3 broadcast_in_dim.125
  219.1 82.7 %while.29 = (s32[]{:T(128)}, f32[4,128,2,128]{1,3,2,0:T(8,128)S(1)}, f32[56,128,128]{2,1,0:T(8,128)}, f32[56,128,128]{2,1,0:T(8,128)}, s32[]{:T(128)}, /*index=5...) while((s32[]{:T(128)}, ...), condition=%wide.region_13.14_spmd.clone, body=%wide.region_10.13_spmd.clone.sunk | while | flops 1354503936 | bytes 46250480 | solution.py:178
  219.7 2.4 compare_and_fusion.5
  222.1 2.2 gather_fusion.2
  224.3 2.2 gather_fusion.1
  226.6 2.4 fusion.87
  229.8 2.1 fusion.91
  233.3 7.1 %scatter_fusion.1 = f32[56,128,128]{2,1,0:T(8,128)} fusion(f32[56,128,128]{2,1,0:T(8,128)} %get-tuple-element.625, s32[32]{0:T(128)S(1)} %fusion.90, f32[32,128,128]{2,1,0:T(8,128)} %bitcast.237), kind=kCustom, calls=%fused_computation.6.clone.clone.1 | custom fusion | flops 524288 | bytes 6291584 | tf_op jit(solution)/shard_map/while/body/scatter-add | solution.py:172
  240.3 6.2 scatter_fusion
  247.2 2.4 compare_and_fusion.5
  249.5 2.2 gather_fusion.2
  251.8 2.2 gather_fusion.1
  254.1 2.4 fusion.87
  257.3 2.1 fusion.91
  260.8 7.0 %scatter_fusion.1 = f32[56,128,128]{2,1,0:T(8,128)} fusion(f32[56,128,128]{2,1,0:T(8,128)} %get-tuple-element.625, s32[32]{0:T(128)S(1)} %fusion.90, f32[32,128,128]{2,1,0:T(8,128)} %bitcast.237), kind=kCustom, calls=%fused_computation.6.clone.clone.1 | custom fusion | flops 524288 | bytes 6291584 | tf_op jit(solution)/shard_map/while/body/scatter-add | solution.py:172
  267.7 6.1 scatter_fusion
  274.4 2.4 compare_and_fusion.5
  276.8 2.2 gather_fusion.2
  279.0 2.2 gather_fusion.1
  281.3 2.4 fusion.87
  284.5 2.1 fusion.91
  288.0 7.2 %scatter_fusion.1 = f32[56,128,128]{2,1,0:T(8,128)} fusion(f32[56,128,128]{2,1,0:T(8,128)} %get-tuple-element.625, s32[32]{0:T(128)S(1)} %fusion.90, f32[32,128,128]{2,1,0:T(8,128)} %bitcast.237), kind=kCustom, calls=%fused_computation.6.clone.clone.1 | custom fusion | flops 524288 | bytes 6291584 | tf_op jit(solution)/shard_map/while/body/scatter-add | solution.py:172
  295.1 6.7 scatter_fusion
  302.3 15.1 %all_to_all.107 = bf16[512,2,128]{2,1,0:T(2,128)(2,1)S(1)} all-to-all(bf16[512,2,128]{2,1,0:T(2,128)(2,1)S(1)} %copy.65), channel_id=1, replica_groups=mesh['ctx'=8,'head'=32] {'head'}, dimensions={0} | all-to-all | bytes 524288 | tf_op jit(solution)/shard_map/all_to_all | solution.py:230
  317.4 167.9 %all_to_all.108 = f32[8,7,128,128]{3,2,1,0:T(8,128)} all-to-all(f32[8,7,128,128]{3,2,1,0:T(8,128)} %bitcast.242), channel_id=1, replica_groups=mesh['ctx'=8,'head'=32] {'ctx'}, dimensions={0} | all-to-all | bytes 7340032 | tf_op jit(solution)/shard_map/all_to_all | solution.py:189
  485.3 4.5 all-to-all-start.10
  489.9 2.5 broadcast_in_dim.134.clone
  492.4 13.3 %scatter_fusion.2 = f32[64,128,128]{2,1,0:T(8,128)} fusion(f32[64,128,128]{2,1,0:T(8,128)} %broadcast_in_dim.134.clone, s32[56]{0:T(128)S(1)} %fusion.36, f32[56,128,128]{2,1,0:T(8,128)} %bitcast.246), kind=kCustom, calls=%fused_computation.7 | custom fusion | flops 917504 | bytes 11010272 | tf_op jit(solution)/shard_map/scatter-add | solution.py:205
  505.7 65.7 %all-to-all-done.10 = f32[8,7,128,128]{3,2,1,0:T(8,128)} async-done(((f32[8,7,128,128]{3,2,1,0:T(8,128)}), f32[8,7,128,128]{3,2,1,0:T(8,128)}, u32[]{:S(2)}, u32[]{:S(2)}) %all-to-all-start.10) | async-done | bytes 3670048 | tf_op jit(solution)/shard_map/all_to_all | solution.py:196
  571.3 8.9 %all-to-all-start.9 = ((f32[32,2,128,128]{3,2,1,0:T(8,128)}), f32[32,2,128,128]{3,2,1,0:T(8,128)}, u32[]{:S(2)}, u32[]{:S(2)}) async-start(f32[32,2,128,128]{3,2,1,0:T(8,128)} %bitcast.244), calls=%async_computation.9 | async-start | bytes 8388608 | tf_op jit(solution)/shard_map/all_to_all | solution.py:208
  580.2 2.5 broadcast_in_dim.134.clone.1
  582.7 13.0 %scatter_fusion.3 = f32[64,128,128]{2,1,0:T(8,128)} fusion(f32[64,128,128]{2,1,0:T(8,128)} %broadcast_in_dim.134.clone.1, s32[56]{0:T(128)S(1)} %fusion.36, f32[56,128,128]{2,1,0:T(8,128)} %bitcast.37), kind=kCustom, calls=%fused_computation.8 | custom fusion | flops 917504 | bytes 11010272 | tf_op jit(solution)/shard_map/scatter-add | solution.py:206
  595.7 36.8 %all-to-all-done.9 = f32[32,2,128,128]{3,2,1,0:T(8,128)} async-done(((f32[32,2,128,128]{3,2,1,0:T(8,128)}), f32[32,2,128,128]{3,2,1,0:T(8,128)}, u32[]{:S(2)}, u32[]{:S(2)}) %all-to-all-start.9) | async-done | bytes 4194336 | tf_op jit(solution)/shard_map/all_to_all | solution.py:208
  632.5 7.2 %all-to-all-start.11 = ((f32[32,2,128,128]{3,2,1,0:T(8,128)}), f32[32,2,128,128]{3,2,1,0:T(8,128)}, u32[]{:S(2)}, u32[]{:S(2)}) async-start(f32[32,2,128,128]{3,2,1,0:T(8,128)} %bitcast.243), calls=%async_computation.11 | async-start | bytes 8388608 | tf_op jit(solution)/shard_map/all_to_all | solution.py:215
  640.5 3.5 bitcast_reduce_fusion.1
  644.0 47.9 %all-to-all-done.11 = f32[32,2,128,128]{3,2,1,0:T(8,128)} async-done(((f32[32,2,128,128]{3,2,1,0:T(8,128)}), f32[32,2,128,128]{3,2,1,0:T(8,128)}, u32[]{:S(2)}, u32[]{:S(2)}) %all-to-all-start.11) | async-done | bytes 4194336 | tf_op jit(solution)/shard_map/all_to_all | solution.py:215
  691.9 3.5 bitcast_reduce_fusion
  (155 shorter events, 25.3 us)
Async XLA Ops:
  2.5 17.6 %all-to-all-start.2 = ((bf16[16,64,128]{2,0,1:T(8,128)(2,1)}), bf16[16,64,128]{2,0,1:T(8,128)(2,1)S(1)}, u32[]{:S(2)}, u32[]{:S(2)}) async-start(bf16[16,64,128]{2,0,1:T(8,128)(2,1)} %copy.54), calls=%async_computation.2 | async-start | bytes 524288 | tf_op jit(solution)/shard_map/all_to_all | solution.py:75
  20.0 12.8 %all-to-all-start.6 = ((bf16[16,64,128]{2,0,1:T(8,128)(2,1)}), bf16[16,64,128]{2,0,1:T(8,128)(2,1)S(1)}, u32[]{:S(2)}, u32[]{:S(2)}) async-start(bf16[16,64,128]{2,0,1:T(8,128)(2,1)} %copy.59), calls=%async_computation.6 | async-start | bytes 524288 | tf_op jit(solution)/shard_map/all_to_all | solution.py:77
  24.9 53.7 %copy-start = (bf16[8,2,1,128,128]{4,3,2,1,0:T(8,128)(2,1)S(1)}, bf16[8,2,1,128,128]{4,3,2,1,0:T(8,128)(2,1)}, u32[]{:S(2)}) copy-start(bf16[8,2,1,128,128]{4,3,2,1,0:T(8,128)(2,1)} %param.13) | copy-start | bytes 1572868
  80.4 32.2 %all-to-all-start.3 = ((bf16[32,2,128,128]{3,2,1,0:T(8,128)(2,1)}), bf16[32,2,128,128]{3,2,1,0:T(8,128)(2,1)S(1)}, u32[]{:S(2)}, u32[]{:S(2)}) async-start(bf16[32,2,128,128]{3,2,1,0:T(8,128)(2,1)} %bitcast.14), calls=%async_computation.3 | async-start | bytes 4194304 | tf_op jit(solution)/shard_map/all_to_all | solution.py:84
  112.7 54.3 %all-to-all-start.1 = ((bf16[8,7,128,128]{3,2,1,0:T(8,128)(2,1)}), bf16[8,7,128,128]{3,2,1,0:T(8,128)(2,1)}, u32[]{:S(2)}, u32[]{:S(2)}) async-start(bf16[8,7,128,128]{3,2,1,0:T(8,128)(2,1)} %bitcast.250), calls=%async_computation.1 | async-start | bytes 3670016 | tf_op jit(solution)/shard_map/all_to_all | solution.py:111
  167.0 47.5 %all-to-all-start.4 = ((bf16[8,7,128,128]{3,2,1,0:T(8,128)(2,1)}), bf16[8,7,128,128]{3,2,1,0:T(8,128)(2,1)}, u32[]{:S(2)}, u32[]{:S(2)}) async-start(bf16[8,7,128,128]{3,2,1,0:T(8,128)(2,1)} %bitcast.251), calls=%async_computation.4 | async-start | bytes 3670016 | tf_op jit(solution)/shard_map/all_to_all | solution.py:112
  485.3 86.0 %all-to-all-start.10 = ((f32[8,7,128,128]{3,2,1,0:T(8,128)}), f32[8,7,128,128]{3,2,1,0:T(8,128)}, u32[]{:S(2)}, u32[]{:S(2)}) async-start(f32[8,7,128,128]{3,2,1,0:T(8,128)} %bitcast.241), calls=%async_computation.10 | async-start | bytes 7340032 | tf_op jit(solution)/shard_map/all_to_all | solution.py:196
  571.3 61.2 %all-to-all-start.9 = ((f32[32,2,128,128]{3,2,1,0:T(8,128)}), f32[32,2,128,128]{3,2,1,0:T(8,128)}, u32[]{:S(2)}, u32[]{:S(2)}) async-start(f32[32,2,128,128]{3,2,1,0:T(8,128)} %bitcast.244), calls=%async_computation.9 | async-start | bytes 8388608 | tf_op jit(solution)/shard_map/all_to_all | solution.py:208
  632.5 59.4 %all-to-all-start.11 = ((f32[32,2,128,128]{3,2,1,0:T(8,128)}), f32[32,2,128,128]{3,2,1,0:T(8,128)}, u32[]{:S(2)}, u32[]{:S(2)}) async-start(f32[32,2,128,128]{3,2,1,0:T(8,128)} %bitcast.243), calls=%async_computation.11 | async-start | bytes 8388608 | tf_op jit(solution)/shard_map/all_to_all | solution.py:215
where the time goes:
time: 700 us; the launch traced here: 695 us
  waiting for transfers between devices  249 us (36%)
  blocking collectives  227 us (32%)
  other arithmetic  93.9 us (13%)
  local copies, waits for them, and re-layouts  51.9 us (7%)
  starting transfers between devices  49.3 us (7%)
  matrix products  22.2 us (3%)
    all_to_all x1, blocking collectives, body(): lax.all_to_all(grad_kf.reshape(ctx_count, capacity, blk_len, head_dim), '...  168 us
    all_to_all x1, waiting for transfers between devices, body(): lax.all_to_all(grad_vf.reshape(ctx_count, capacity, blk_len, head_dim), '...  65.7 us
    all_to_all x1, waiting for transfers between devices, body(): lax.all_to_all(grad_v_held.reshape(head_count, per_dev, blk_len, head_dim...  47.9 us
    all_to_all x1, waiting for transfers between devices, body(): lax.all_to_all(key_held[send_ids], 'ctx', split_axis=0, concat_axis=0, ti...  40.1 us
    all_to_all x1, waiting for transfers between devices, body(): lax.all_to_all(grad_k_held.reshape(head_count, per_dev, blk_len, head_dim...  36.8 us
    all_to_all x1, blocking collectives, body(): lax.all_to_all(key_send, 'head', split_axis=0, concat_axis=1, tiled=True)  31.8 us
    all_to_all x1, waiting for transfers between devices, body(): lax.all_to_all(value_held[send_ids], 'ctx', split_axis=0, concat_axis=0,...  24.8 us
    scatter-add x3, other arithmetic, grad_turn(): grad_vf.at[flat_slots]  21.2 us
  transfers between devices with their start and end apart: 8, of which 8 were waited for; matrix products, arithmetic and copies ran while one was open for 10% of the time, Pallas kernels for 0%

commit v1 on v0

v1 whole, which is shorter than its diff:
```python
import functools

import jax
import jax.numpy as jnp
from jax import lax
from jax.experimental import pallas as pl
from jax.experimental.pallas import tpu as pltpu
from jax.sharding import PartitionSpec as P

MESH = pl.DeviceIdType.MESH
VMEM = pltpu.VMEM
SMEM = pltpu.SMEM
NEG = -1e30
LOG2E = 1.4426950408889634
LANES = 128
FAR = 4096


def whole(space):
    return pl.BlockSpec(memory_space=space)


def nt(a, b):
    return lax.dot_general(a, b, (((1,), (1,)), ((), ())), preferred_element_type=jnp.float32)


def nn(a, b):
    return lax.dot_general(a, b, (((1,), (0,)), ((), ())), preferred_element_type=jnp.float32)


def iota(shape, dim):
    return lax.broadcasted_iota(jnp.int32, shape, dim)


def plan_kernel(dims, lists_ref, counts_ref, ids_ref, thr_ref, inv_ref):
    n_ctx, members, per_group, own, cap = dims
    g = lax.axis_index("ctx")
    h = lax.axis_index("head") // members
    blocks, kv, slots = lists_ref.shape
    total = n_ctx * per_group
    pick = iota((blocks, kv, slots), 1) == h
    lists = jnp.sum(jnp.where(pick, lists_ref[...].astype(jnp.float32), 0.0), axis=1)
    count = jnp.sum(
        jnp.where(iota((blocks, kv), 1) == h, counts_ref[...].astype(jnp.float32), 0.0),
        axis=1,
        keepdims=True,
    )
    lists = jnp.where(iota((blocks, slots), 1).astype(jnp.float32) < count, lists, -1.0)
    col = iota((1, total), 1)
    col_id = ((col % per_group) * n_ctx + col // per_group).astype(jnp.float32)
    live = jnp.zeros((blocks, total), jnp.float32)
    for n in range(slots):
        live = jnp.where(lists[:, n : n + 1] == col_id, 1.0, live)
    low = live.astype(jnp.bfloat16)
    of_group = (iota((8, blocks), 1) // own == iota((8, blocks), 0)).astype(jnp.float32)
    used = nn(of_group.astype(jnp.bfloat16), low) > 0.5
    used_f = used.astype(jnp.float32)
    before = (iota((total, total), 0) // per_group == iota((total, total), 1) // per_group) & (
        iota((total, total), 0) < iota((total, total), 1)
    )
    place = nn(used_f.astype(jnp.bfloat16), before.astype(jnp.float32).astype(jnp.bfloat16))
    rows8 = iota((8, blocks), 0)
    own_rows = ((iota((8, blocks), 1) == own * g + rows8) & (rows8 < own)).astype(jnp.float32)
    own_live = nn(own_rows.astype(jnp.bfloat16), low)
    row8 = iota((8, total), 0)
    diag = (
        (col_id == (total - blocks + own * g + row8).astype(jnp.float32)) & (row8 < own)
    ).astype(jnp.float32)
    key_row = iota((total, 2 * LANES), 0)
    lane = iota((total, 2 * LANES), 1)
    key_group = key_row // per_group
    key_local = key_row % per_group
    got = jnp.zeros((24, 2 * LANES), jnp.float32)
    for k in range(cap):
        match = jnp.where(used & (place == k), 1.0, 0.0)
        mine = jnp.sum(jnp.where(row8 == g, match, 0.0), axis=0, keepdims=True)
        left = jnp.concatenate([match, own_live * mine, diag * mine], axis=0)
        right = jnp.where(
            lane == k,
            jnp.where(key_group == g, key_local, 0),
            jnp.where(lane == LANES + k * n_ctx + key_group, 1, 0),
        )
        got = got + nn(left.astype(jnp.bfloat16), right.astype(jnp.float32).astype(jnp.bfloat16))
    ids_ref[...] = got[0:8, :LANES].astype(jnp.int32)
    is_live = got[8:16, LANES:] > 0.5
    is_diag = got[16:24, LANES:] > 0.5
    thr_ref[...] = jnp.where(is_diag & is_live, 0, jnp.where(is_live, -FAR, FAR))
    held_at = ((iota((total, LANES), 0) // per_group == g)
               & (iota((total, LANES), 0) % per_group == iota((total, LANES), 1)))
    back = nn(
        jnp.where(used, place, float(cap)).astype(jnp.bfloat16),
        held_at.astype(jnp.float32).astype(jnp.bfloat16),
    )
    inv_ref[...] = back.astype(jnp.int32)


def greet(g, d, n_ctx, n_head):
    barrier = pltpu.get_barrier_semaphore()

    def plane(o, _):
        pl.semaphore_signal(
            barrier, inc=1, device_id=(g, lax.rem(d + o, n_head)), device_id_type=MESH
        )
        return 0

    lax.fori_loop(1, n_head, plane, 0)

    def line(o, _):
        pl.semaphore_signal(
            barrier, inc=1, device_id=(lax.rem(g + o, n_ctx), d), device_id_type=MESH
        )
        return 0

    lax.fori_loop(1, n_ctx, line, 0)
    pl.semaphore_wait(barrier, n_head + n_ctx - 2)


def await_bytes(ref, sem):
    pltpu.make_async_copy(ref, ref, sem).wait()


def spread_kernel(
    dims,
    ids,
    q,
    do,
    dl,
    keys,
    vals,
    k_got,
    v_got,
    q_got,
    do_got,
    dl_got,
    k_held,
    v_held,
    k_send,
    v_send,
    ss,
    rs,
):
    n_ctx, n_head, members, per_dev, quarter, cap = dims
    g = lax.axis_index("ctx")
    d = lax.axis_index("head")
    greet(g, d, n_ctx, n_head)

    def held_pair(src, p, held):
        return (
            src.at[p // members, :, 0, pl.ds((p % members) * quarter, quarter), :],
            held.at[pl.ds(per_dev * d, per_dev)],
        )

    def send(src, dst, n, to):
        pltpu.make_async_remote_copy(
            src_ref=src,
            dst_ref=dst,
            send_sem=ss.at[n],
            recv_sem=rs.at[n],
            device_id=to,
            device_id_type=MESH,
        ).start()

    def send_kv(o, _):
        p = lax.rem(d + o, n_head)
        send(*held_pair(keys, p, k_held), 0, (g, p))
        send(*held_pair(vals, p, v_held), 1, (g, p))
        return 0

    lax.fori_loop(1, n_head, send_kv, 0)
    pltpu.make_async_copy(*held_pair(keys, d, k_held), rs.at[0]).start()
    pltpu.make_async_copy(*held_pair(vals, d, v_held), rs.at[1]).start()

    def send_q(o, _):
        p = lax.rem(d + o, n_head)
        h = p // members
        send(q.at[h], q_got.at[d], 2, (g, p))
        send(do.at[h], do_got.at[d], 3, (g, p))
        send(dl.at[h], dl_got.at[d], 4, (g, p))
        return 0

    lax.fori_loop(1, n_head, send_q, 0)
    h = d // members
    pltpu.make_async_copy(q.at[h], q_got.at[d], rs.at[2]).start()
    pltpu.make_async_copy(do.at[h], do_got.at[d], rs.at[3]).start()
    pltpu.make_async_copy(dl.at[h], dl_got.at[d], rs.at[4]).start()

    for n, held, packed, out in ((0, k_held, k_send, k_got), (1, v_held, v_send, v_got)):
        await_bytes(held, rs.at[n])

        def pack(c, _, held=held, packed=packed):
            for k in range(cap):
                packed[c, k] = held[ids[c, k]]
            return 0

        lax.fori_loop(0, n_ctx, pack, 0)

        def send_line(o, _, packed=packed, out=out, n=n):
            c = lax.rem(g + o, n_ctx)
            send(packed.at[c], out.at[g], 5 + n, (c, d))
            return 0

        lax.fori_loop(1, n_ctx, send_line, 0)
        pltpu.make_async_copy(packed.at[g], out.at[g], rs.at[5 + n]).start()

    for n, ref in ((2, q_got), (3, do_got), (4, dl_got), (5, k_got), (6, v_got)):
        await_bytes(ref, rs.at[n])
    for n, ref in ((0, k_held), (1, v_held)):
        await_bytes(ref.at[pl.ds(0, per_dev * (n_head - 1))], ss.at[n])
    for n, ref in ((2, q_got), (3, do_got), (4, dl_got)):
        await_bytes(ref.at[pl.ds(0, n_head - 1)], ss.at[n])
    for n, ref in ((5, k_got), (6, v_got)):
        await_bytes(ref.at[pl.ds(0, n_ctx - 1)], ss.at[n])


def share_kernel(dims, stats, got, ss, rs):
    members = dims
    g = lax.axis_index("ctx")
    d = lax.axis_index("head")
    first = (d // members) * members
    me = d % members
    barrier = pltpu.get_barrier_semaphore()
    for o in range(1, members):
        pl.semaphore_signal(
            barrier, inc=1, device_id=(g, first + lax.rem(me + o, members)), device_id_type=MESH
        )
    pl.semaphore_wait(barrier, members - 1)
    for o in range(1, members):
        pltpu.make_async_remote_copy(
            src_ref=stats,
            dst_ref=got.at[me],
            send_sem=ss,
            recv_sem=rs,
            device_id=(g, first + lax.rem(me + o, members)),
            device_id_type=MESH,
        ).start()
    pltpu.make_async_copy(stats, got.at[me], rs).start()
    await_bytes(got, rs)
    await_bytes(got.at[pl.ds(0, members - 1)], ss)


def gather_kernel(
    dims,
    inv,
    gq,
    gk,
    gv,
    gq_out,
    gk_out,
    gv_out,
    gq_got,
    k_back,
    v_back,
    k_sum,
    v_sum,
    ss,
    rs,
):
    n_ctx, n_head, members, per_dev, quarter, cap = dims
    g = lax.axis_index("ctx")
    d = lax.axis_index("head")
    h = d // members
    m = d % members
    greet(g, d, n_ctx, n_head)

    def send(src, dst, n, to):
        pltpu.make_async_remote_copy(
            src_ref=src,
            dst_ref=dst,
            send_sem=ss.at[n],
            recv_sem=rs.at[n],
            device_id=to,
            device_id_type=MESH,
        ).start()

    for n, src, back in ((0, gk, k_back), (1, gv, v_back)):

        def send_line(o, _, src=src, back=back, n=n):
            c = lax.rem(g + o, n_ctx)
            send(src.at[c], back.at[g, pl.ds(0, cap)], n, (c, d))
            return 0

        lax.fori_loop(1, n_ctx, send_line, 0)
        pltpu.make_async_copy(src.at[g], back.at[g, pl.ds(0, cap)], rs.at[n]).start()

    def send_q(o, _):
        p = lax.rem(d + o, n_head)
        send(gq.at[p], gq_got.at[d], 2, (g, p))
        return 0

    lax.fori_loop(1, n_head, send_q, 0)
    pltpu.make_async_copy(gq.at[d], gq_got.at[d], rs.at[2]).start()

    for n, src, back, total, out in (
        (0, gk, k_back, k_sum, gk_out),
        (1, gv, v_back, v_sum, gv_out),
    ):
        for c in range(n_ctx):
            back[c, cap] = jnp.zeros(back.shape[2:], back.dtype)
        await_bytes(src, rs.at[n])

        def add_up(l, _, back=back, total=total):
            acc = back[0, inv[0, l]].astype(jnp.float32)
            for c in range(1, n_ctx):
                acc = acc + back[c, inv[c, l]].astype(jnp.float32)
            total[l] = acc.astype(total.dtype)
            return 0

        lax.fori_loop(0, per_dev * n_head, add_up, 0)

        def place(out=out):
            return out.at[h, :, 0, pl.ds(m * quarter, quarter), :]

        def send_home(o, _, total=total, n=n, place=place):
            p = lax.rem(d + o, n_head)
            send(total.at[pl.ds(per_dev * p, per_dev)], place(), 3 + n, (g, p))
            return 0

        lax.fori_loop(1, n_head, send_home, 0)
        pltpu.make_async_copy(total.at[pl.ds(per_dev * d, per_dev)], place(), rs.at[3 + n]).start()

    await_bytes(gq_got, rs.at[2])

    def add_q(e, _):
        acc = gq_got[members * e].astype(jnp.float32)
        for o in range(1, members):
            acc = acc + gq_got[members * e + o].astype(jnp.float32)
        gq_out[e] = acc.astype(gq_out.dtype)
        return 0

    lax.fori_loop(0, n_head // members, add_q, 0)
    await_bytes(k_sum, rs.at[3])
    await_bytes(v_sum, rs.at[4])
    for n, ref in ((0, gk), (1, gv)):
        await_bytes(ref.at[pl.ds(0, n_ctx - 1)], ss.at[n])
    await_bytes(gq.at[pl.ds(0, n_head - 1)], ss.at[2])
    for n, ref in ((3, k_sum), (4, v_sum)):
        await_bytes(ref.at[pl.ds(0, per_dev * (n_head - 1))], ss.at[n])


def reach(rows, quarter, m):
    shape = (quarter, rows)
    return iota(shape, 1) // 8 - iota(shape, 0) - m * quarter


def scaled(thr, i, c, n_ctx, cap, quarter, gap, raw):
    factor = (LANES ** -0.5) * LOG2E
    parts = []
    for k in range(cap):
        part = raw[k * quarter : (k + 1) * quarter] * factor
        parts.append(jnp.where(gap >= thr[i, k * n_ctx + c], part, NEG))
    return jnp.concatenate(parts, axis=0)


def stats_kernel(dims, thr, k_got, q_got, stats):
    n_ctx, members, quarter, cap, own, rows = dims
    m = lax.axis_index("head") % members
    gap = reach(rows, quarter, m)

    def one(i, _):
        def step(c, carry):
            top, mass = carry
            raw = nt(k_got[pl.ds(c * cap * quarter, cap * quarter)], q_got[pl.ds(i * rows, rows)])
            score = scaled(thr, i, c, n_ctx, cap, quarter, gap, raw)
            new = jnp.maximum(top, jnp.max(score, axis=0, keepdims=True))
            mass = mass * jnp.exp2(top - new) + jnp.sum(
                jnp.exp2(score - new), axis=0, keepdims=True
            )
            return new, mass

        top, mass = lax.fori_loop(
            0,
            n_ctx,
            step,
            (jnp.full((1, rows), NEG, jnp.float32), jnp.zeros((1, rows), jnp.float32)),
        )
        stats[pl.ds(i, 1)] = top
        stats[pl.ds(4 + i, 1)] = mass
        return 0

    lax.fori_loop(0, own, one, 0)


def grads_kernel(dims, thr, shared, dl_got, k_got, v_got, q_got, do_got, gq, gk, gv, lse, delta, gq_t):
    n_ctx, members, quarter, cap, own, rows = dims
    m = lax.axis_index("head") % members
    gap = reach(rows, quarter, m)
    c = pl.program_id(0)
    scaling = LANES ** -0.5

    @pl.when(c == 0)
    def _():
        gq_t[...] = jnp.zeros_like(gq_t)
        for i in range(own):
            tops = [shared[e, i : i + 1] for e in range(members)]
            top = functools.reduce(jnp.maximum, tops)
            mass = sum(shared[e, 4 + i : 5 + i] * jnp.exp2(tops[e] - top) for e in range(members))
            lse[i : i + 1] = top + jnp.log2(mass)
            per = rows // LANES
            delta[i : i + 1] = jnp.concatenate([dl_got[i * per + e] for e in range(per)], axis=1)

    keys = k_got[0]
    vals = v_got[0]
    keys_t = keys.T

    def one(i, carry):
        acc_k, acc_v = carry
        q = q_got[pl.ds(i * rows, rows)]
        do = do_got[pl.ds(i * rows, rows)]
        score = scaled(thr, i, c, n_ctx, cap, quarter, gap, nt(keys, q))
        prob = jnp.exp2(score - lse[pl.ds(i, 1)])
        dprob = nt(vals, do)
        dscore = (prob * (dprob - delta[pl.ds(i, 1)])).astype(jnp.bfloat16)
        acc_v = acc_v + nn(prob.astype(jnp.bfloat16), do)
        acc_k = acc_k + nn(dscore, q)
        gq_t[i] += nn(keys_t, dscore)
        return acc_k, acc_v

    zero = jnp.zeros((cap * quarter, LANES), jnp.float32)
    acc_k, acc_v = lax.fori_loop(0, own, one, (zero, zero))
    gk[0] = (acc_k * scaling).astype(gk.dtype)
    gv[0] = acc_v.astype(gv.dtype)

    @pl.when(c == n_ctx - 1)
    def _():
        for i in range(own):
            gq[i * rows : (i + 1) * rows] = (gq_t[i].T * scaling).astype(gq.dtype)


def body(queries, keys, values, outputs, grad_out, block_ids, block_counts):
    f32, bf16, i32 = jnp.float32, jnp.bfloat16, jnp.int32
    n_ctx = lax.axis_size("ctx")
    n_head = lax.axis_size("head")
    kv, per_dev, _, blk, dh = keys.shape
    tokens, heads, _ = queries.shape
    members = n_head // kv
    quarter = blk // members
    group = heads // kv
    per_group = per_dev * n_head
    blocks, _, slots = block_ids.shape
    own = blocks // n_ctx
    cap = (slots + own + n_ctx - 2) // n_ctx
    part = tokens * group
    rows = blk * group
    any_ = whole(pl.ANY)
    vm = whole(VMEM)
    sm = whole(SMEM)
    limit = 60 * 2**20

    def by_kv(x):
        return jnp.transpose(x.reshape(tokens, kv, group, dh), (1, 0, 2, 3)).reshape(kv, part, dh)

    delta = jnp.sum(grad_out.astype(f32) * outputs.astype(f32), axis=2)
    delta = jnp.transpose(delta.reshape(tokens, kv, group), (1, 0, 2)).reshape(kv, 1, part)
    q8 = by_kv(queries)
    do8 = by_kv(grad_out)

    ids, thr, inv = pl.pallas_call(
        functools.partial(plan_kernel, (n_ctx, members, per_group, own, cap)),
        out_shape=[jax.ShapeDtypeStruct((8, LANES), i32)] * 3,
        in_specs=[vm, vm],
        out_specs=[vm] * 3,
        compiler_params=pltpu.CompilerParams(vmem_limit_bytes=limit),
        name="plan",
    )(block_ids, block_counts)

    comm = (n_ctx, n_head, members, per_dev, quarter, cap)
    packed = (n_ctx, cap, quarter, dh)
    held = (per_group, quarter, dh)
    k_got, v_got, q_got, do_got, dl_got = pl.pallas_call(
        functools.partial(spread_kernel, comm),
        out_shape=[
            jax.ShapeDtypeStruct(packed, bf16),
            jax.ShapeDtypeStruct(packed, bf16),
            jax.ShapeDtypeStruct((n_head, part, dh), bf16),
            jax.ShapeDtypeStruct((n_head, part, dh), bf16),
            jax.ShapeDtypeStruct((n_head, 1, part), f32),
        ],
        in_specs=[sm] + [any_] * 5,
        out_specs=[any_] * 5,
        scratch_shapes=[
            VMEM(held, bf16),
            VMEM(held, bf16),
            VMEM(packed, bf16),
            VMEM(packed, bf16),
            pltpu.SemaphoreType.DMA((7,)),
            pltpu.SemaphoreType.DMA((7,)),
        ],
        compiler_params=pltpu.CompilerParams(
            collective_id=0, has_side_effects=True, vmem_limit_bytes=16 * 2**20
        ),
        name="spread",
    )(ids, q8, do8, delta, keys, values)

    comp = (n_ctx, members, quarter, cap, own, rows)
    keys_own = k_got.reshape(n_ctx * cap * quarter, dh)
    q_rows = q_got.reshape(n_head * part, dh)
    do_rows = do_got.reshape(n_head * part, dh)
    stats = pl.pallas_call(
        functools.partial(stats_kernel, comp),
        out_shape=jax.ShapeDtypeStruct((8, rows), f32),
        in_specs=[sm, vm, vm],
        out_specs=vm,
        compiler_params=pltpu.CompilerParams(vmem_limit_bytes=limit),
        name="stats",
    )(thr, keys_own, q_rows)

    shared = pl.pallas_call(
        functools.partial(share_kernel, members),
        out_shape=jax.ShapeDtypeStruct((members, 8, rows), f32),
        in_specs=[vm],
        out_specs=vm,
        scratch_shapes=[pltpu.SemaphoreType.DMA, pltpu.SemaphoreType.DMA],
        compiler_params=pltpu.CompilerParams(
            collective_id=1, has_side_effects=True, vmem_limit_bytes=16 * 2**20
        ),
        name="share",
    )(stats)

    chunk = (n_ctx, cap * quarter, dh)
    block = pl.BlockSpec((1, cap * quarter, dh), lambda c: (c, 0, 0))
    gq, gk, gv = pl.pallas_call(
        functools.partial(grads_kernel, comp),
        grid=(n_ctx,),
        out_shape=[
            jax.ShapeDtypeStruct((n_head * part, dh), bf16),
            jax.ShapeDtypeStruct(chunk, bf16),
            jax.ShapeDtypeStruct(chunk, bf16),
        ],
        in_specs=[sm, vm, vm, block, block, vm, vm],
        out_specs=[vm, block, block],
        scratch_shapes=[
            VMEM((own, rows), f32),
            VMEM((own, rows), f32),
            VMEM((own, dh, rows), f32),
        ],
        compiler_params=pltpu.CompilerParams(vmem_limit_bytes=limit),
        name="grads",
    )(thr, shared, dl_got, k_got.reshape(chunk), v_got.reshape(chunk), q_rows, do_rows)

    back = (n_ctx, cap + 1, quarter, dh)
    gq8, grad_keys, grad_values = pl.pallas_call(
        functools.partial(gather_kernel, comm),
        out_shape=[
            jax.ShapeDtypeStruct((kv, part, dh), bf16),
            jax.ShapeDtypeStruct(keys.shape, bf16),
            jax.ShapeDtypeStruct(keys.shape, bf16),
        ],
        in_specs=[sm, any_, any_, any_],
        out_specs=[vm, any_, any_],
        scratch_shapes=[
            VMEM((n_head, part, dh), bf16),
            VMEM(back, bf16),
            VMEM(back, bf16),
            VMEM(held, bf16),
            VMEM(held, bf16),
            pltpu.SemaphoreType.DMA((5,)),
            pltpu.SemaphoreType.DMA((5,)),
        ],
        compiler_params=pltpu.CompilerParams(
            collective_id=2, has_side_effects=True, vmem_limit_bytes=16 * 2**20
        ),
        name="gather",
    )(inv, gq.reshape(n_head, part, dh), gk.reshape(packed), gv.reshape(packed))
    grad_queries = jnp.transpose(gq8.reshape(kv, tokens, group, dh), (1, 0, 2, 3)).reshape(
        tokens, heads, dh
    )
    return grad_queries, grad_keys, grad_values


def solution(mesh):
    tok = P(("ctx", "head"), None, None)
    cached = P(None, "head", "ctx", None, None)
    return jax.shard_map(
        body,
        mesh=mesh,
        in_specs=(tok, cached, cached, tok, tok, P(), P()),
        out_specs=(tok, cached, cached),
        check_vma=False,
    )
```

time: 700 us -> 174 us (0.25)
  waiting for transfers between devices: 249 us -> 0 us
  blocking collectives: 227 us -> 0 us
  Pallas kernels: 0 us -> 158 us
  other arithmetic: 93.9 us -> 1.28 us
  starting transfers between devices: 49.3 us -> 0 us
  local copies, waits for them, and re-layouts: 51.9 us -> 13.9 us
  matrix products: 22.2 us -> 0 us
    all_to_all x8 -> x0, waiting for transfers between devices: 249 us -> none  [the longest x1 65.7 us: body(): lax.all_to_all(grad_vf.reshape(ctx_count, capacity, blk_len, head_dim), '...]
    all_to_all x4 -> x0, blocking collectives: 227 us -> none  [the longest x1 168 us: body(): lax.all_to_all(grad_kf.reshape(ctx_count, capacity, blk_len, head_dim), '...]
    pallas_call x0 -> x6, Pallas kernels: none -> 158 us  [the longest x1 52.3 us: body(): pl.pallas_call(functools.partial(gather_kernel, comm), out_shape=[jax.Sha...]
    scatter-add x8 -> x0, other arithmetic: 66.5 us -> none  [the longest x3 21.2 us: grad_turn(): grad_vf.at[flat_slots]]
    all_to_all x8 -> x0, starting transfers between devices: 49.3 us -> none  [the longest x1 8.88 us: body(): lax.all_to_all(grad_k_held.reshape(head_count, per_dev, blk_len, head_dim...]
    gather x11 -> x0, local copies, waits for them, and re-layouts: 26 us -> none  [the longest x6 13.5 us: turn_inputs(): key_part = key_got[slots].reshape(own_blocks, slot_step * blk_len, head_dim)]
    dot_general x18 -> x0, matrix products: 22.2 us -> none  [the longest x6 9.57 us: masked_scores(): jnp.einsum('kqhd,ksd->khqs', query_part, key_part, preferred_element_type...]
    broadcast_in_dim x15 -> x0, local copies, waits for them, and re-layouts: 13.5 us -> none  [the longest x2 4.98 us: body(): zero_rows = jnp.zeros((per_group, blk_len, head_dim), jnp.float32)]
  transfers between devices with their start and end apart: 8 -> 0, of which waited for: 8 -> 0; matrix products, arithmetic and copies ran while one was open for 10% -> 0% of each run, Pallas kernels for 0% -> 0%
where the time goes in v1:
time: 174 us
  Pallas kernels  158 us (91%)
  local copies, waits for them, and re-layouts  13.9 us (8%)
    pallas_call x1, Pallas kernels, body(): pl.pallas_call(functools.partial(gather_kernel, comm), out_shape=[jax.Sha...  52.3 us
    pallas_call x1, Pallas kernels, body(): pl.pallas_call(functools.partial(spread_kernel, comm), out_shape=[jax.Sha...  50.3 us
    pallas_call x1, Pallas kernels, body(): pl.pallas_call(functools.partial(grads_kernel, comp), grid=(n_ctx,), out_...  30.8 us
    pallas_call x1, Pallas kernels, body(): pl.pallas_call(functools.partial(stats_kernel, comp), out_shape=jax.Shape...  16.3 us
    unnamed x37, local copies, waits for them, and re-layouts  12.8 us
    pallas_call x1, Pallas kernels, body(): pl.pallas_call(functools.partial(share_kernel, members), out_shape=jax.Sh...  5.31 us

profile of v1, /device:TPU:1, one launch (start us, length us, event | category | flops | bytes accessed | tf_op | source)
XLA Modules:
  0.0 173.8 jit_solution(1907112005819634785)
XLA Ops:
  0.6 0.0 copy-start
  0.6 0.0 copy-start.16
  0.7 1.3 multiply_reduce_fusion
  1.9 0.0 copy-done.16
  2.0 0.0 copy-start.15
  2.0 0.7 copy.20.counts_ref
  2.6 2.7 %plan.1 = (s32[8,128]{1,0:T(8,128)}, s32[8,128]{1,0:T(8,128)}, s32[8,128]{1,0:T(8,128)}) custom-call(s32[32,8,48]{2,1,0:T(8,128)} %lists_ref.1, s32[32,8]{1,0:T(8,128)} %copy.20.counts_ref), custom_call_target="tpu_custom_call" | custom-call | tf_op jit(solution)/shard_map/plan/pallas_call | solution.py:457
  5.4 0.1 copy.23
  5.4 0.1 copy.24
  5.5 0.0 copy-start.14
  5.5 0.1 reshape.59
  5.6 0.0 copy-done
  5.6 0.0 copy-done.15
  5.6 0.0 copy-start.5
  5.7 0.0 copy-start.6
  5.7 0.1 copy_bitcast_fusion.1
  5.8 0.4 copy-done.14
  6.2 0.5 copy-done.5
  6.7 0.2 copy-done.6
  6.8 50.3 %spread.1 = (bf16[8,7,32,128]{3,2,1,0:T(8,128)(2,1)S(1)}, bf16[8,7,32,128]{3,2,1,0:T(8,128)(2,1)S(1)}, bf16[32,128,128]{2,1,0:T(8,128)(2,1)S(1)}, bf16[32,128,128]{2,1,0:T(8,128)(2,1)S(1)}, f32[32,1,128]{2,1,0:T(1,128)S(1)}) custom-call(s32[8,128]{1,0:T(8,128)S(1)} %copy-done.14, bf16[8,128,128]{2,1,0:T(8,128)(2,1)S(1)} %get-tuple-element.32.q, ...), custom_call_target="tpu_custom_call" | custom-call | tf_op jit(solution)/shard_map/spread/pallas_call | solution.py:469
  57.2 0.0 copy-start.1
  57.2 1.0 copy-done.1
  58.2 0.0 copy-start.2
  58.2 0.8 copy-done.2
  58.9 0.0 copy-start.3
  58.9 1.0 copy-done.3
  59.9 0.0 copy-start.8
  59.9 0.8 copy-done.8
  60.7 0.0 copy-start.12
  60.7 0.6 copy-done.12
  61.3 16.3 %stats.1 = f32[8,1024]{1,0:T(8,128)} custom-call(s32[8,128]{1,0:T(8,128)} %get-tuple-element.18.thr, bf16[1792,128]{1,0:T(8,128)(2,1)} %bitcast.35, bf16[4096,128]{1,0:T(8,128)(2,1)} %bitcast.33), custom_call_target="tpu_custom_call" | custom-call | tf_op jit(solution)/shard_map/stats/pallas_call | solution.py:498
  77.6 0.0 copy-start.11
  77.6 0.8 copy-done.11
  78.4 5.3 %share.1.shared = f32[4,8,1024]{2,1,0:T(8,128)S(1)} custom-call(f32[8,1024]{1,0:T(8,128)S(1)} %copy-done.11), custom_call_target="tpu_custom_call" | custom-call | tf_op jit(solution)/shard_map/share/pallas_call | solution.py:507
  83.7 0.0 copy-start.7
  83.7 0.6 copy-done.7
  84.3 30.8 %grads.1 = (bf16[4096,128]{1,0:T(8,128)(2,1)}, bf16[8,224,128]{2,1,0:T(8,128)(2,1)}, bf16[8,224,128]{2,1,0:T(8,128)(2,1)}) custom-call(s32[8,128]{1,0:T(8,128)} %get-tuple-element.18.thr, f32[4,8,1024]{2,1,0:T(8,128)} %copy-done.7, f32[32,1,128]{2,1,0:T(1,128)} %copy-done.12, bf16[8,224,128]{2,1,0:T(8,128)(2,1)} %bitcast.36, bf16[8,224,128]{2,1,0:T(8,128)(2,1)} %bitcast.39, ...), custom_call_target="tpu_custom_call" | custom-call | tf_op jit(solution)/shard_map/grads/pallas_call | solution.py:521
  115.2 0.0 copy-start.13
  115.2 0.7 copy-done.13
  115.9 0.0 copy-start.4
  115.9 1.2 copy-done.4
  117.1 0.0 copy-start.9
  117.1 1.0 copy-done.9
  118.1 0.0 copy-start.10
  118.1 1.0 copy-done.10
  119.1 52.3 %gather.1 = (bf16[8,128,128]{2,1,0:T(8,128)(2,1)S(1)}, bf16[8,2,1,128,128]{4,3,2,1,0:T(8,128)(2,1)S(1)}, bf16[8,2,1,128,128]{4,3,2,1,0:T(8,128)(2,1)S(1)}) custom-call(s32[8,128]{1,0:T(8,128)S(1)} %copy-done.13, bf16[32,128,128]{2,1,0:T(8,128)(2,1)S(1)} %bitcast.38, bf16[8,7,32,128]{3,2,1,0:T(8,128)(2,1)S(1)} %bitcast.40, bf16[8,7,32,128]{3,2,1,0:T(8,128)(2,1)S(1)} %bitcast.41), custom_call_target="tpu_custom_call" | custom-call | tf_op jit(solution)/shard_map/gather/pallas_call | solution.py:541
  171.5 0.8 copy_bitcast_fusion
  172.2 0.8 copy.32
  173.0 0.8 copy.33
Async XLA Ops:
  0.6 5.0 %copy-start = (bf16[16,64,128]{2,1,0:T(8,128)(2,1)S(1)}, bf16[16,64,128]{2,1,0:T(8,128)(2,1)}, u32[]{:S(2)}) copy-start(bf16[16,64,128]{2,1,0:T(8,128)(2,1)} %param.7) | copy-start | bytes 786436
  0.6 1.3 copy-start.16
  2.0 3.7 %copy-start.15 = (bf16[16,64,128]{2,1,0:T(8,128)(2,1)S(1)}, bf16[16,64,128]{2,1,0:T(8,128)(2,1)}, u32[]{:S(2)}) copy-start(bf16[16,64,128]{2,1,0:T(8,128)(2,1)} %param.11) | copy-start | bytes 786436
  5.5 0.7 copy-start.14
  5.6 1.0 copy-start.5
  5.7 1.2 copy-start.6
  57.2 1.0 copy-start.1
  58.2 0.8 copy-start.2
  58.9 1.0 copy-start.3
  59.9 0.8 copy-start.8
  60.7 0.6 copy-start.12
  77.6 0.8 copy-start.11
  83.7 0.7 copy-start.7
  115.2 0.7 copy-start.13
  115.9 1.2 copy-start.4
  117.1 1.0 copy-start.9
  118.1 1.0 copy-start.10

commit v2 on v1

v2 whole, which is shorter than its diff:
```python
import functools

import jax
import jax.numpy as jnp
from jax import lax
from jax.experimental import pallas as pl
from jax.experimental.pallas import tpu as pltpu
from jax.sharding import PartitionSpec as P

MESH = pl.DeviceIdType.MESH
VMEM = pltpu.VMEM
SMEM = pltpu.SMEM
NEG = -1e30
LOG2E = 1.4426950408889634
LANES = 128
FAR = 4096


def whole(space):
    return pl.BlockSpec(memory_space=space)


def nt(a, b):
    return lax.dot_general(a, b, (((1,), (1,)), ((), ())), preferred_element_type=jnp.float32)


def nn(a, b):
    return lax.dot_general(a, b, (((1,), (0,)), ((), ())), preferred_element_type=jnp.float32)


def iota(shape, dim):
    return lax.broadcasted_iota(jnp.int32, shape, dim)


def plan_kernel(dims, lists_ref, counts_ref, ids_ref, thr_ref, inv_ref):
    n_ctx, members, per_group, own, cap = dims
    g = lax.axis_index("ctx")
    h = lax.axis_index("head") // members
    blocks, kv, slots = lists_ref.shape
    total = n_ctx * per_group
    pick = iota((blocks, kv, slots), 1) == h
    lists = jnp.sum(jnp.where(pick, lists_ref[...].astype(jnp.float32), 0.0), axis=1)
    count = jnp.sum(
        jnp.where(iota((blocks, kv), 1) == h, counts_ref[...].astype(jnp.float32), 0.0),
        axis=1,
        keepdims=True,
    )
    lists = jnp.where(iota((blocks, slots), 1).astype(jnp.float32) < count, lists, -1.0)
    col = iota((1, total), 1)
    col_id = ((col % per_group) * n_ctx + col // per_group).astype(jnp.float32)
    live = jnp.zeros((blocks, total), jnp.float32)
    for n in range(slots):
        live = jnp.where(lists[:, n : n + 1] == col_id, 1.0, live)
    low = live.astype(jnp.bfloat16)
    of_group = (iota((8, blocks), 1) // own == iota((8, blocks), 0)).astype(jnp.float32)
    used = nn(of_group.astype(jnp.bfloat16), low) > 0.5
    used_f = used.astype(jnp.float32)
    before = (iota((total, total), 0) // per_group == iota((total, total), 1) // per_group) & (
        iota((total, total), 0) < iota((total, total), 1)
    )
    place = nn(used_f.astype(jnp.bfloat16), before.astype(jnp.float32).astype(jnp.bfloat16))
    rows8 = iota((8, blocks), 0)
    own_rows = ((iota((8, blocks), 1) == own * g + rows8) & (rows8 < own)).astype(jnp.float32)
    own_live = nn(own_rows.astype(jnp.bfloat16), low)
    row8 = iota((8, total), 0)
    diag = (
        (col_id == (total - blocks + own * g + row8).astype(jnp.float32)) & (row8 < own)
    ).astype(jnp.float32)
    key_row = iota((total, 2 * LANES), 0)
    lane = iota((total, 2 * LANES), 1)
    key_group = key_row // per_group
    key_local = key_row % per_group
    got = jnp.zeros((24, 2 * LANES), jnp.float32)
    for k in range(cap):
        match = jnp.where(used & (place == k), 1.0, 0.0)
        mine = jnp.sum(jnp.where(row8 == g, match, 0.0), axis=0, keepdims=True)
        left = jnp.concatenate([match, own_live * mine, diag * mine], axis=0)
        right = jnp.where(
            lane == k,
            jnp.where(key_group == g, key_local, 0),
            jnp.where(lane == LANES + k * n_ctx + key_group, 1, 0),
        )
        got = got + nn(left.astype(jnp.bfloat16), right.astype(jnp.float32).astype(jnp.bfloat16))
    ids_ref[...] = got[0:8, :LANES].astype(jnp.int32)
    is_live = got[8:16, LANES:] > 0.5
    is_diag = got[16:24, LANES:] > 0.5
    thr_ref[...] = jnp.where(is_diag & is_live, 0, jnp.where(is_live, -FAR, FAR))
    held_at = ((iota((total, LANES), 0) // per_group == g)
               & (iota((total, LANES), 0) % per_group == iota((total, LANES), 1)))
    back = nn(
        jnp.where(used, place, float(cap)).astype(jnp.bfloat16),
        held_at.astype(jnp.float32).astype(jnp.bfloat16),
    )
    inv_ref[...] = back.astype(jnp.int32)


def greet(g, d, n_ctx, n_head):
    barrier = pltpu.get_barrier_semaphore()

    def plane(o, _):
        pl.semaphore_signal(
            barrier, inc=1, device_id=(g, lax.rem(d + o, n_head)), device_id_type=MESH
        )
        return 0

    lax.fori_loop(1, n_head, plane, 0)

    def line(o, _):
        pl.semaphore_signal(
            barrier, inc=1, device_id=(lax.rem(g + o, n_ctx), d), device_id_type=MESH
        )
        return 0

    lax.fori_loop(1, n_ctx, line, 0)
    pl.semaphore_wait(barrier, n_head + n_ctx - 2)


def await_bytes(ref, sem):
    pltpu.make_async_copy(ref, ref, sem).wait()


def near_first(s, n):
    return lax.rem((s % 2) * ((s + 1) // 2) + (1 - s % 2) * (n - s // 2), n)


def far_first(s, n):
    return n // 2 + ((s + 1) // 2) * (1 - 2 * (s % 2))


def reach(rows, quarter, m):
    shape = (quarter, rows)
    return iota(shape, 1) // 8 - iota(shape, 0) - m * quarter


def scaled(thr, i, c, n_ctx, cap, quarter, gap, raw):
    factor = (LANES ** -0.5) * LOG2E
    parts = []
    for k in range(cap):
        part = raw[k * quarter : (k + 1) * quarter] * factor
        parts.append(jnp.where(gap >= thr[i, k * n_ctx + c], part, NEG))
    return jnp.concatenate(parts, axis=0)


def main_kernel(
    dims,
    ids,
    thr,
    inv,
    q,
    do,
    dl,
    keys,
    vals,
    gq_out,
    gk_out,
    gv_out,
    k_held,
    v_held,
    k_send,
    v_send,
    k_got,
    v_got,
    q_got,
    do_got,
    dl_got,
    weights,
    tops,
    stats,
    shared,
    lse,
    delta,
    gq_t,
    gq_send,
    gq_got,
    gk_send,
    gv_send,
    k_back,
    v_back,
    k_acc,
    v_acc,
    k_sum,
    v_sum,
    ss,
    rs,
    rs_line,
):
    n_ctx, n_head, members, per_dev, quarter, cap, own, rows = dims
    g = lax.axis_index("ctx")
    d = lax.axis_index("head")
    h = d // members
    m = d % members
    core = d % 2
    chip = d // 2
    chips = n_head // 2
    partner = 2 * chip + 1 - core
    per = rows // LANES
    scaling = LANES ** -0.5
    greet(g, d, n_ctx, n_head)

    def send(src, dst, s_sem, r_sem, to):
        pltpu.make_async_remote_copy(
            src_ref=src,
            dst_ref=dst,
            send_sem=s_sem,
            recv_sem=r_sem,
            device_id=to,
            device_id_type=MESH,
        ).start()

    def held_pair(src, p, held):
        return (
            src.at[p // members, :, 0, pl.ds((p % members) * quarter, quarter), :],
            held.at[pl.ds(per_dev * d, per_dev)],
        )

    for n, src, held in ((0, keys, k_held), (1, vals, v_held)):

        def send_kv(o, _, n=n, src=src, held=held):
            p = lax.rem(d + o, n_head)
            send(*held_pair(src, p, held), ss.at[n], rs.at[n], (g, p))
            return 0

        lax.fori_loop(1, n_head, send_kv, 0)
        pltpu.make_async_copy(*held_pair(src, d, held), rs.at[n]).start()

    def send_q(o, _):
        t = lax.rem(chip + o, chips)
        send(q.at[2 * t // members], q_got.at[d], ss.at[2], rs.at[2], (g, 2 * t))
        send(do.at[2 * t // members], do_got.at[d], ss.at[2], rs.at[3], (g, 2 * t + 1))
        return 0

    lax.fori_loop(1, chips, send_q, 0)

    @pl.when(core == 0)
    def _():
        pltpu.make_async_copy(q.at[h], q_got.at[d], rs.at[2]).start()
        send(do.at[h], do_got.at[d], ss.at[2], rs.at[3], (g, partner))

    @pl.when(core == 1)
    def _():
        pltpu.make_async_copy(do.at[h], do_got.at[d], rs.at[3]).start()
        send(q.at[h], q_got.at[d], ss.at[2], rs.at[2], (g, partner))

    def send_d(o, _):
        p = lax.rem(d + o, n_head)
        send(dl.at[p // members], dl_got.at[d], ss.at[4], rs.at[4], (g, p))
        return 0

    lax.fori_loop(1, n_head, send_d, 0)
    pltpu.make_async_copy(dl.at[h], dl_got.at[d], rs.at[4]).start()

    for n, held, packed, out in ((0, k_held, k_send, k_got), (1, v_held, v_send, v_got)):
        await_bytes(held, rs.at[n])

        def pack(s, _, n=n, held=held, packed=packed, out=out):
            off = near_first(s, n_ctx)
            c = lax.rem(g + off, n_ctx)
            for k in range(cap):
                packed[c, k] = held[ids[c, k]]

            @pl.when(s > 0)
            def _():
                send(packed.at[c], out.at[g], ss.at[5 + n], rs_line.at[n, off], (c, d))

            @pl.when(s == 0)
            def _():
                pltpu.make_async_copy(packed.at[c], out.at[g], rs_line.at[n, off]).start()

            return 0

        lax.fori_loop(0, n_ctx, pack, 0)

    @pl.when(core == 0)
    def _():
        await_bytes(q_got, rs.at[2])
        send(q_got, q_got, ss.at[3], rs.at[2], (g, partner))

    @pl.when(core == 1)
    def _():
        await_bytes(do_got, rs.at[3])
        send(do_got, do_got, ss.at[3], rs.at[3], (g, partner))
        await_bytes(q_got, rs.at[2])

    gap = reach(rows, quarter, m)
    stats[...] = jnp.where(iota(stats.shape, 0) < 4, NEG, 0.0)

    def weigh(s, _):
        off = near_first(s, n_ctx)
        c = lax.rem(g - off + n_ctx, n_ctx)
        await_bytes(k_got.at[c], rs_line.at[0, off])

        def one(i, _):
            key = k_got[c].reshape(cap * quarter, LANES)
            query = q_got[pl.ds(i * per, per)].reshape(rows, LANES)
            score = scaled(thr, i, c, n_ctx, cap, quarter, gap, nt(key, query))
            old = stats[pl.ds(i, 1)]
            new = jnp.maximum(old, jnp.max(score, axis=0, keepdims=True))
            weight = jnp.exp2(score - new)
            weights[c, i] = weight
            tops[c, pl.ds(i, 1)] = new
            stats[pl.ds(i, 1)] = new
            stats[pl.ds(4 + i, 1)] = stats[pl.ds(4 + i, 1)] * jnp.exp2(old - new) + jnp.sum(
                weight, axis=0, keepdims=True
            )
            return 0

        lax.fori_loop(0, own, one, 0)
        return 0

    lax.fori_loop(0, n_ctx, weigh, 0)

    for o in range(1, members):
        to = (g, h * members + lax.rem(m + o, members))
        send(stats, shared.at[m], ss.at[7], rs.at[5], to)
    pltpu.make_async_copy(stats, shared.at[m], rs.at[5]).start()

    @pl.when(core == 0)
    def _():
        await_bytes(do_got, rs.at[3])

    await_bytes(dl_got, rs.at[4])
    for i in range(own):
        delta[i : i + 1] = jnp.concatenate([dl_got[i * per + e] for e in range(per)], axis=1)
    gq_t[...] = jnp.zeros_like(gq_t)
    await_bytes(shared, rs.at[5])
    for i in range(own):
        each = [shared[e, i : i + 1] for e in range(members)]
        top = functools.reduce(jnp.maximum, each)
        mass = sum(shared[e, 4 + i : 5 + i] * jnp.exp2(each[e] - top) for e in range(members))
        lse[i : i + 1] = top + jnp.log2(mass)

    def grads(s, _):
        off = far_first(s, n_ctx)
        c = lax.rem(g + off, n_ctx)
        await_bytes(v_got.at[c], rs_line.at[1, lax.rem(n_ctx - off, n_ctx)])
        key = k_got[c].reshape(cap * quarter, LANES)
        value = v_got[c].reshape(cap * quarter, LANES)
        key_t = key.T

        def one(i, carry):
            acc_k, acc_v = carry
            query = q_got[pl.ds(i * per, per)].reshape(rows, LANES)
            cot = do_got[pl.ds(i * per, per)].reshape(rows, LANES)
            prob = weights[c, i] * jnp.exp2(tops[c, pl.ds(i, 1)] - lse[pl.ds(i, 1)])
            dscore = (prob * (nt(value, cot) - delta[pl.ds(i, 1)])).astype(jnp.bfloat16)
            acc_v = acc_v + nn(prob.astype(jnp.bfloat16), cot)
            acc_k = acc_k + nn(dscore, query)
            gq_t[i] += nn(key_t, dscore)
            return acc_k, acc_v

        zero = jnp.zeros((cap * quarter, LANES), jnp.float32)
        acc_k, acc_v = lax.fori_loop(0, own, one, (zero, zero))
        gk_send[c] = (acc_k * scaling).astype(gk_send.dtype).reshape(cap, quarter, LANES)
        gv_send[c] = acc_v.astype(gv_send.dtype).reshape(cap, quarter, LANES)
        for n, packed, back in ((0, gk_send, k_back), (1, gv_send, v_back)):
            for e in range(n_ctx):

                @pl.when(off == e)
                def _(n=n, packed=packed, place=back[e].at[pl.ds(0, cap)], e=e):
                    if e > 0:
                        send(packed.at[c], place, ss.at[8 + n], rs_line.at[2 + n, e], (c, d))
                    else:
                        pltpu.make_async_copy(packed.at[c], place, rs_line.at[2 + n, e]).start()

        return 0

    lax.fori_loop(0, n_ctx, grads, 0)

    def turn(i, _):
        part = (gq_t[i].T * scaling).astype(gq_send.dtype)
        gq_send[pl.ds(i * per, per)] = part.reshape(per, LANES, LANES)
        return 0

    lax.fori_loop(0, own, turn, 0)

    def send_gq(o, _):
        p = lax.rem(d + o, n_head)
        send(gq_send.at[p], gq_got.at[d], ss.at[10], rs.at[6], (g, p))
        return 0

    lax.fori_loop(1, n_head, send_gq, 0)
    pltpu.make_async_copy(gq_send.at[d], gq_got.at[d], rs.at[6]).start()

    for c in range(n_ctx):
        k_back[c][cap] = jnp.zeros(k_back[c].shape[1:], k_back[c].dtype)
        v_back[c][cap] = jnp.zeros(v_back[c].shape[1:], v_back[c].dtype)

    def picked(back, offs, l):
        acc = None
        for off in offs:
            c = lax.rem(g - off + n_ctx, n_ctx)
            term = back[off][inv[c, l]].astype(jnp.float32)
            acc = term if acc is None else acc + term
        return acc

    half = n_ctx // 2
    pairs = [(0, half)] + [(half - e, half + e) for e in range(1, half)]
    for step, offs in enumerate(pairs):
        for off in offs:
            c = lax.rem(g - off + n_ctx, n_ctx)
            await_bytes(gk_send.at[c], rs_line.at[2, off])
            await_bytes(gv_send.at[c], rs_line.at[3, off])
        if step < len(pairs) - 1:

            def add_up(l, _, offs=offs, step=step):
                for back, acc in ((k_back, k_acc), (v_back, v_acc)):
                    term = picked(back, offs, l)
                    acc[l] = term if step == 0 else acc[l] + term
                return 0

            lax.fori_loop(0, per_dev * n_head, add_up, 0)
        else:

            def finish(o, _, offs=offs):
                p = lax.rem(d + o, n_head)
                for n, back, acc, total, out in (
                    (0, k_back, k_acc, k_sum, gk_out),
                    (1, v_back, v_acc, v_sum, gv_out),
                ):
                    for e in range(per_dev):
                        l = per_dev * p + e
                        total[l] = (acc[l] + picked(back, offs, l)).astype(total.dtype)
                    src = total.at[pl.ds(per_dev * p, per_dev)]
                    place = out.at[h, :, 0, pl.ds(m * quarter, quarter), :]

                    @pl.when(o < n_head)
                    def _(n=n, src=src, place=place):
                        send(src, place, ss.at[11 + n], rs.at[7 + n], (g, p))

                    @pl.when(o == n_head)
                    def _(n=n, src=src, place=place):
                        pltpu.make_async_copy(src, place, rs.at[7 + n]).start()

                return 0

            lax.fori_loop(1, n_head + 1, finish, 0)

    await_bytes(gq_got, rs.at[6])

    def add_q(e, _):
        acc = gq_got[members * e].astype(jnp.float32)
        for o in range(1, members):
            acc = acc + gq_got[members * e + o].astype(jnp.float32)
        gq_out[e] = acc.astype(gq_out.dtype)
        return 0

    lax.fori_loop(0, n_head // members, add_q, 0)
    await_bytes(k_sum, rs.at[7])
    await_bytes(v_sum, rs.at[8])
    for n, ref in ((0, k_held), (1, v_held), (11, k_sum), (12, v_sum)):
        await_bytes(ref.at[pl.ds(0, per_dev * (n_head - 1))], ss.at[n])
    for n, ref in ((2, q_got), (4, dl_got), (10, gq_send)):
        await_bytes(ref.at[pl.ds(0, n_head - 1)], ss.at[n])
    await_bytes(q_got, ss.at[3])
    for n, ref in ((5, k_send), (6, v_send), (8, gk_send), (9, gv_send)):
        await_bytes(ref.at[pl.ds(0, n_ctx - 1)], ss.at[n])
    await_bytes(shared.at[pl.ds(0, members - 1)], ss.at[7])


def body(queries, keys, values, outputs, grad_out, block_ids, block_counts):
    f32, bf16, i32 = jnp.float32, jnp.bfloat16, jnp.int32
    n_ctx = lax.axis_size("ctx")
    n_head = lax.axis_size("head")
    kv, per_dev, _, blk, dh = keys.shape
    tokens, heads, _ = queries.shape
    members = n_head // kv
    quarter = blk // members
    group = heads // kv
    per_group = per_dev * n_head
    blocks, _, slots = block_ids.shape
    own = blocks // n_ctx
    cap = (slots + own + n_ctx - 2) // n_ctx
    part = tokens * group
    rows = blk * group
    any_ = whole(pl.ANY)
    vm = whole(VMEM)
    sm = whole(SMEM)
    limit = 60 * 2**20

    def by_kv(x):
        return jnp.transpose(x.reshape(tokens, kv, group, dh), (1, 0, 2, 3)).reshape(kv, part, dh)

    delta = jnp.sum(grad_out.astype(f32) * outputs.astype(f32), axis=2)
    delta = jnp.transpose(delta.reshape(tokens, kv, group), (1, 0, 2)).reshape(kv, 1, part)
    q8 = by_kv(queries)
    do8 = by_kv(grad_out)

    ids, thr, inv = pl.pallas_call(
        functools.partial(plan_kernel, (n_ctx, members, per_group, own, cap)),
        out_shape=[jax.ShapeDtypeStruct((8, LANES), i32)] * 3,
        in_specs=[vm, vm],
        out_specs=[vm] * 3,
        compiler_params=pltpu.CompilerParams(vmem_limit_bytes=limit),
        name="plan",
    )(block_ids, block_counts)

    packed = (n_ctx, cap, quarter, dh)
    back = [VMEM((cap + 1, quarter, dh), bf16)] * n_ctx
    held = (per_group, quarter, dh)
    spread = (n_head, part, dh)
    gq8, grad_keys, grad_values = pl.pallas_call(
        functools.partial(
            main_kernel, (n_ctx, n_head, members, per_dev, quarter, cap, own, rows)
        ),
        out_shape=[
            jax.ShapeDtypeStruct((kv, part, dh), bf16),
            jax.ShapeDtypeStruct(keys.shape, bf16),
            jax.ShapeDtypeStruct(keys.shape, bf16),
        ],
        in_specs=[sm] * 3 + [any_] * 5,
        out_specs=[vm, any_, any_],
        scratch_shapes=[
            VMEM(held, bf16),
            VMEM(held, bf16),
            VMEM(packed, bf16),
            VMEM(packed, bf16),
            VMEM(packed, bf16),
            VMEM(packed, bf16),
            VMEM(spread, bf16),
            VMEM(spread, bf16),
            VMEM((n_head, 1, part), f32),
            VMEM((n_ctx, own, cap * quarter, rows), f32),
            VMEM((n_ctx, own, rows), f32),
            VMEM((8, rows), f32),
            VMEM((members, 8, rows), f32),
            VMEM((own, rows), f32),
            VMEM((own, rows), f32),
            VMEM((own, dh, rows), f32),
            VMEM(spread, bf16),
            VMEM(spread, bf16),
            VMEM(packed, bf16),
            VMEM(packed, bf16),
            back,
            back,
            VMEM(held, f32),
            VMEM(held, f32),
            VMEM(held, bf16),
            VMEM(held, bf16),
            pltpu.SemaphoreType.DMA((13,)),
            pltpu.SemaphoreType.DMA((9,)),
            pltpu.SemaphoreType.DMA((4, n_ctx)),
        ],
        compiler_params=pltpu.CompilerParams(
            collective_id=0, has_side_effects=True, vmem_limit_bytes=limit
        ),
        name="main",
    )(ids, thr, inv, q8, do8, delta, keys, values)
    grad_queries = jnp.transpose(gq8.reshape(kv, tokens, group, dh), (1, 0, 2, 3)).reshape(
        tokens, heads, dh
    )
    return grad_queries, grad_keys, grad_values


def solution(mesh):
    tok = P(("ctx", "head"), None, None)
    cached = P(None, "head", "ctx", None, None)
    return jax.shard_map(
        body,
        mesh=mesh,
        in_specs=(tok, cached, cached, tok, tok, P(), P()),
        out_specs=(tok, cached, cached),
        check_vma=False,
    )
```

time: 174 us -> 121 us (0.70)
  Pallas kernels: 158 us -> 112 us
  local copies, waits for them, and re-layouts: 13.9 us -> 6.28 us
    pallas_call x5 -> x1, Pallas kernels: 155 us -> 109 us  [body(): pl.pallas_call(functools.partial(main_kernel, (n_ctx, n_head, members, pe...]
    unnamed x37 -> x13, local copies, waits for them, and re-layouts: 12.8 us -> 2.73 us
where the time goes in v2:
time: 121 us; the launch traced here: 120 us
  Pallas kernels  112 us (93%)
  local copies, waits for them, and re-layouts  6.28 us (5%)
  other arithmetic  1.28 us (1%)
    pallas_call x1, Pallas kernels, body(): pl.pallas_call(functools.partial(main_kernel, (n_ctx, n_head, members, pe...  109 us
    unnamed x13, local copies, waits for them, and re-layouts  2.73 us
    pallas_call x1, Pallas kernels, body(): pl.pallas_call(functools.partial(plan_kernel, (n_ctx, members, per_group,...  2.7 us

profile of v2, /device:TPU:1, one launch (start us, length us, event | category | flops | bytes accessed | tf_op | source)
XLA Modules:
  0.0 119.9 jit_solution(6918082322934121760)
XLA Ops:
  0.6 0.0 copy-start
  0.6 0.0 copy-start.4
  0.7 1.3 %multiply_reduce_fusion = f32[16,64]{1,0:T(8,128)S(1)} fusion(bf16[16,64,128]{2,1,0:T(8,128)(2,1)} %param.10, bf16[16,64,128]{2,1,0:T(8,128)(2,1)} %param.11), kind=kLoop, calls=%fused_computation | loop fusion | flops 523264 | bytes 528384 | tf_op jit(solution)/shard_map/reduce_sum | solution.py:483
  1.9 0.0 copy-done.4
  2.0 0.0 copy-start.1
  2.0 0.7 copy.20.counts_ref
  2.6 2.7 %plan.1 = (s32[8,128]{1,0:T(8,128)}, s32[8,128]{1,0:T(8,128)}, s32[8,128]{1,0:T(8,128)}) custom-call(s32[32,8,48]{2,1,0:T(8,128)} %lists_ref.1, s32[32,8]{1,0:T(8,128)} %copy.20.counts_ref), custom_call_target="tpu_custom_call" | custom-call | tf_op jit(solution)/shard_map/plan/pallas_call | solution.py:488
  5.3 0.1 copy.23
  5.4 0.1 copy.24
  5.5 0.7 reshape.35
  6.2 0.0 copy-done
  6.2 0.0 copy-done.1
  6.2 0.9 copy_bitcast_fusion.1
  7.1 108.9 %main.1 = (bf16[8,128,128]{2,1,0:T(8,128)(2,1)}, bf16[8,2,1,128,128]{4,3,2,1,0:T(8,128)(2,1)}, bf16[8,2,1,128,128]{4,3,2,1,0:T(8,128)(2,1)}) custom-call(s32[8,128]{1,0:T(8,128)} %get-tuple-element.9.ids, s32[8,128]{1,0:T(8,128)} %get-tuple-element.10.thr, s32[8,128]{1,0:T(8,128)} %get-tuple-element.11.inv, bf16[8,128,128]{2,1,0:T(8,128)(2,1)} %get-tuple-element.16.q, ...), custom_call_target="tpu_custom_call" | custom-call | tf_op jit(solution)/shard_map/main/pallas_call | solution.py:501
  116.1 0.0 copy-start.3
  116.1 1.8 %copy_bitcast_fusion = bf16[16,64,128]{2,1,0:T(8,128)(2,1)} fusion(bf16[8,128,128]{2,1,0:T(8,128)(2,1)} %get-tuple-element.12), kind=kLoop, calls=%fused_computation.1 | loop fusion | bytes 524288 | tf_op jit(solution)/shard_map/reshape | solution.py:548
  117.9 0.0 copy-done.3
  117.9 0.0 copy-start.2
  117.9 0.8 copy.32
  118.7 0.4 copy-done.2
  119.1 0.8 copy.33
Async XLA Ops:
  0.6 5.6 %copy-start = (bf16[16,64,128]{2,1,0:T(8,128)(2,1)S(1)}, bf16[16,64,128]{2,1,0:T(8,128)(2,1)}, u32[]{:S(2)}) copy-start(bf16[16,64,128]{2,1,0:T(8,128)(2,1)} %param.7) | copy-start | bytes 786436
  0.6 1.3 %copy-start.4 = (s32[32,8]{0,1:T(8,128)S(1)}, s32[32,8]{0,1:T(8,128)}, u32[]{:S(2)}) copy-start(s32[32,8]{0,1:T(8,128)} %param.13) | copy-start | bytes 3076
  2.0 4.3 %copy-start.1 = (bf16[16,64,128]{2,1,0:T(8,128)(2,1)S(1)}, bf16[16,64,128]{2,1,0:T(8,128)(2,1)}, u32[]{:S(2)}) copy-start(bf16[16,64,128]{2,1,0:T(8,128)(2,1)} %param.11) | copy-start | bytes 786436
  116.1 1.8 %copy-start.3 = (bf16[8,2,1,128,128]{4,3,2,1,0:T(8,128)(2,1)S(1)}, bf16[8,2,1,128,128]{4,3,2,1,0:T(8,128)(2,1)}, u32[]{:S(2)}) copy-start(bf16[8,2,1,128,128]{4,3,2,1,0:T(8,128)(2,1)} %get-tuple-element.21) | copy-start | bytes 1572868
  117.9 1.2 %copy-start.2 = (bf16[8,2,1,128,128]{4,3,2,1,0:T(8,128)(2,1)S(1)}, bf16[8,2,1,128,128]{4,3,2,1,0:T(8,128)(2,1)}, u32[]{:S(2)}) copy-start(bf16[8,2,1,128,128]{4,3,2,1,0:T(8,128)(2,1)} %get-tuple-element.22) | copy-start | bytes 1572868

commit v3 on v2

v3 whole, which is shorter than its diff:
```python
import functools

import jax
import jax.numpy as jnp
from jax import lax
from jax.experimental import pallas as pl
from jax.experimental.pallas import tpu as pltpu
from jax.sharding import PartitionSpec as P

MESH = pl.DeviceIdType.MESH
VMEM = pltpu.VMEM
SMEM = pltpu.SMEM
NEG = -1e30
LOG2E = 1.4426950408889634
LANES = 128
FAR = 4096
HOOK = 2
HOOK_SUM = 6


def whole(space):
    return pl.BlockSpec(memory_space=space)


def nt(a, b):
    return lax.dot_general(a, b, (((1,), (1,)), ((), ())), preferred_element_type=jnp.float32)


def nn(a, b):
    return lax.dot_general(a, b, (((1,), (0,)), ((), ())), preferred_element_type=jnp.float32)


def iota(shape, dim):
    return lax.broadcasted_iota(jnp.int32, shape, dim)


def plan(dims, lists_ref, counts_ref, ids_ref, thr_ref, inv_ref):
    n_ctx, members, per_group, own, cap = dims
    g = lax.axis_index("ctx")
    h = lax.axis_index("head") // members
    blocks, kv, slots = lists_ref.shape
    total = n_ctx * per_group
    pick = iota((blocks, kv, slots), 1) == h
    lists = jnp.sum(jnp.where(pick, lists_ref[...].astype(jnp.float32), 0.0), axis=1)
    count = jnp.sum(
        jnp.where(iota((kv, blocks), 0) == h, counts_ref[...].astype(jnp.float32), 0.0),
        axis=0,
        keepdims=True,
    )
    square = iota((blocks, blocks), 0) == iota((blocks, blocks), 1)
    count = jnp.sum(jnp.where(square, count, 0.0), axis=1, keepdims=True)
    lists = jnp.where(iota((blocks, slots), 1).astype(jnp.float32) < count, lists, -1.0)
    col = iota((1, total), 1)
    col_id = ((col % per_group) * n_ctx + col // per_group).astype(jnp.float32)
    live = jnp.zeros((blocks, total), jnp.float32)
    for n in range(slots):
        live = jnp.where(lists[:, n : n + 1] == col_id, 1.0, live)
    low = live.astype(jnp.bfloat16)
    of_group = (iota((8, blocks), 1) // own == iota((8, blocks), 0)).astype(jnp.float32)
    used = nn(of_group.astype(jnp.bfloat16), low) > 0.5
    used_f = used.astype(jnp.float32)
    before = (iota((total, total), 0) // per_group == iota((total, total), 1) // per_group) & (
        iota((total, total), 0) < iota((total, total), 1)
    )
    place = nn(used_f.astype(jnp.bfloat16), before.astype(jnp.float32).astype(jnp.bfloat16))
    rows8 = iota((8, blocks), 0)
    own_rows = ((iota((8, blocks), 1) == own * g + rows8) & (rows8 < own)).astype(jnp.float32)
    own_live = nn(own_rows.astype(jnp.bfloat16), low)
    row8 = iota((8, total), 0)
    diag = (
        (col_id == (total - blocks + own * g + row8).astype(jnp.float32)) & (row8 < own)
    ).astype(jnp.float32)
    key_row = iota((total, 2 * LANES), 0)
    lane = iota((total, 2 * LANES), 1)
    key_group = key_row // per_group
    key_local = key_row % per_group
    got = jnp.zeros((24, 2 * LANES), jnp.float32)
    for k in range(cap):
        match = jnp.where(used & (place == k), 1.0, 0.0)
        mine = jnp.sum(jnp.where(row8 == g, match, 0.0), axis=0, keepdims=True)
        left = jnp.concatenate([match, own_live * mine, diag * mine], axis=0)
        right = jnp.where(
            lane == k,
            jnp.where(key_group == g, key_local, 0),
            jnp.where(lane == LANES + k * n_ctx + key_group, 1, 0),
        )
        got = got + nn(left.astype(jnp.bfloat16), right.astype(jnp.float32).astype(jnp.bfloat16))
    ids_ref[...] = got[0:8, :LANES].astype(jnp.int32)
    is_live = got[8:16, LANES:] > 0.5
    is_diag = got[16:24, LANES:] > 0.5
    thr_ref[...] = jnp.where(is_diag & is_live, 0, jnp.where(is_live, -FAR, FAR))
    held_at = ((iota((total, LANES), 0) // per_group == g)
               & (iota((total, LANES), 0) % per_group == iota((total, LANES), 1)))
    back = nn(
        jnp.where(used, place, float(cap)).astype(jnp.bfloat16),
        held_at.astype(jnp.float32).astype(jnp.bfloat16),
    )
    inv_ref[...] = back.astype(jnp.int32)


def greet(g, d, n_ctx, n_head):
    barrier = pltpu.get_barrier_semaphore()

    def plane(o, _):
        pl.semaphore_signal(
            barrier, inc=1, device_id=(g, lax.rem(d + o, n_head)), device_id_type=MESH
        )
        return 0

    lax.fori_loop(1, n_head, plane, 0)

    def line(o, _):
        pl.semaphore_signal(
            barrier, inc=1, device_id=(lax.rem(g + o, n_ctx), d), device_id_type=MESH
        )
        return 0

    lax.fori_loop(1, n_ctx, line, 0)
    pl.semaphore_wait(barrier, n_head + n_ctx - 2)


def await_bytes(ref, sem):
    pltpu.make_async_copy(ref, ref, sem).wait()


def near_first(s, n):
    return lax.rem((s % 2) * ((s + 1) // 2) + (1 - s % 2) * (n - s // 2), n)


def far_first(s, n):
    return n // 2 + ((s + 1) // 2) * (1 - 2 * (s % 2))


def reach(rows, quarter, m):
    shape = (quarter, rows)
    return iota(shape, 1) // 8 - iota(shape, 0) - m * quarter


def scaled(thr, i, c, n_ctx, cap, quarter, gap, raw):
    factor = (LANES ** -0.5) * LOG2E
    parts = []
    for k in range(cap):
        part = raw[k * quarter : (k + 1) * quarter] * factor
        parts.append(jnp.where(gap >= thr[i, k * n_ctx + c], part, NEG))
    return jnp.concatenate(parts, axis=0)


def main_kernel(
    dims,
    lists,
    counts,
    q,
    do,
    out8,
    keys,
    vals,
    gq_out,
    gk_out,
    gv_out,
    plans,
    ids,
    thr,
    inv,
    dl_send,
    k_held,
    v_held,
    k_send,
    v_send,
    k_got,
    v_got,
    q_got,
    do_got,
    dl_got,
    weights,
    tops,
    stats,
    shared,
    lse,
    delta,
    gq_t,
    gq_send,
    gq_pair,
    gq_got,
    gk_send,
    gv_send,
    k_back,
    v_back,
    k_sum,
    v_sum,
    ss,
    rs,
    rs_line,
    local_sem,
):
    n_ctx, n_head, members, per_dev, quarter, cap, own, rows = dims
    g = lax.axis_index("ctx")
    d = lax.axis_index("head")
    h = d // members
    m = d % members
    core = d % 2
    chip = d // 2
    chips = n_head // 2
    partner = 2 * chip + 1 - core
    per = rows // LANES
    half = n_head // 2
    scaling = LANES ** -0.5
    greet(g, d, n_ctx, n_head)

    def send(src, dst, s_sem, r_sem, to):
        pltpu.make_async_remote_copy(
            src_ref=src,
            dst_ref=dst,
            send_sem=s_sem,
            recv_sem=r_sem,
            device_id=to,
            device_id_type=MESH,
        ).start()

    def held_pair(src, p, held):
        return (
            src.at[p // members, :, 0, pl.ds((p % members) * quarter, quarter), :],
            held.at[pl.ds(per_dev * d, per_dev)],
        )

    def send_held(n, src, held):
        def one(o, _):
            p = lax.rem(d + o, n_head)
            send(*held_pair(src, p, held), ss.at[n], rs.at[n], (g, p))
            return 0

        lax.fori_loop(1, n_head, one, 0)
        pltpu.make_async_copy(*held_pair(src, d, held), rs.at[n]).start()

    def held_left(n, held):
        await_bytes(held.at[pl.ds(0, per_dev * (n_head - 1))], ss.at[n])

    def send_rows(src, got, n, to_core):
        def one(o, _):
            t = lax.rem(chip + o, chips)
            send(src.at[2 * t // members], got.at[d], ss.at[n], rs.at[n], (g, 2 * t + to_core))
            return 0

        lax.fori_loop(1, chips, one, 0)

        @pl.when(core == to_core)
        def _():
            pltpu.make_async_copy(src.at[h], got.at[d], rs.at[n]).start()

        @pl.when(core != to_core)
        def _():
            send(src.at[h], got.at[d], ss.at[n], rs.at[n], (g, partner))

    def rows_left(got, n, to_core):
        await_bytes(got.at[pl.ds(0, chips - 1)], ss.at[n])

        @pl.when(core != to_core)
        def _():
            await_bytes(got.at[0], ss.at[n])

    def forward(got, n, to_core):
        @pl.when(core == to_core)
        def _():
            await_bytes(got, rs.at[n])
            send(got, got, ss.at[4], rs.at[n], (g, partner))

    def send_retained(n, held, packed, got):
        await_bytes(held, rs.at[n])

        def one(s, _):
            off = near_first(s, n_ctx)
            c = lax.rem(g + off, n_ctx)
            for k in range(cap):
                packed[c, k] = held[jnp.clip(ids[c, k], 0, per_dev * n_head - 1)]

            @pl.when(s > 0)
            def _():
                send(packed.at[c], got.at[g], ss.at[6 + n], rs_line.at[n, off], (c, d))

            @pl.when(s == 0)
            def _():
                pltpu.make_async_copy(packed.at[c], got.at[g], rs_line.at[n, off]).start()

            return 0

        lax.fori_loop(0, n_ctx, one, 0)

    send_held(0, keys, k_held)

    plan((n_ctx, members, per_dev * n_head, own, cap), lists, counts, *[plans.at[e] for e in range(3)])
    for e, place in enumerate((ids, thr, inv)):
        pltpu.make_async_copy(plans.at[e], place, local_sem.at[e]).start()
    for e in range(n_head // members):
        product = do[e].astype(jnp.float32) * out8[e].astype(jnp.float32)
        dl_send[e] = jnp.sum(product.T, axis=0, keepdims=True)
    for e, place in enumerate((ids, thr, inv)):
        pltpu.make_async_copy(plans.at[e], place, local_sem.at[e]).wait()

    held_left(0, k_held)
    send_rows(q, q_got, 2, 0)
    send_retained(0, k_held, k_send, k_got)
    rows_left(q_got, 2, 0)
    send_held(1, vals, v_held)
    forward(q_got, 2, 0)

    @pl.when(core == 1)
    def _():
        await_bytes(q_got, rs.at[2])

    def more():
        held_left(1, v_held)
        send_rows(do, do_got, 3, 1)

        def send_delta(o, _):
            p = lax.rem(d + o, n_head)
            send(dl_send.at[p // members], dl_got.at[d], ss.at[5], rs.at[4], (g, p))
            return 0

        lax.fori_loop(1, n_head, send_delta, 0)
        pltpu.make_async_copy(dl_send.at[h], dl_got.at[d], rs.at[4]).start()
        send_retained(1, v_held, v_send, v_got)

    gap = reach(rows, quarter, m)
    stats[...] = jnp.where(iota(stats.shape, 0) < 4, NEG, 0.0)

    def weigh(s, _):
        off = near_first(s, n_ctx)
        c = lax.rem(g - off + n_ctx, n_ctx)
        await_bytes(k_got.at[c], rs_line.at[0, off])

        @pl.when(s == HOOK)
        def _():
            more()

        for i in range(own):
            key = k_got[c].reshape(cap * quarter, LANES)
            query = q_got[pl.ds(i * per, per)].reshape(rows, LANES)
            score = scaled(thr, i, c, n_ctx, cap, quarter, gap, nt(key, query))
            old = stats[pl.ds(i, 1)]
            new = jnp.maximum(old, jnp.max(score, axis=0, keepdims=True))
            weight = jnp.exp2(score - new)
            weights[c, i] = weight
            tops[c, pl.ds(i, 1)] = new
            stats[pl.ds(i, 1)] = new
            stats[pl.ds(4 + i, 1)] = stats[pl.ds(4 + i, 1)] * jnp.exp2(old - new) + jnp.sum(
                weight, axis=0, keepdims=True
            )
        return 0

    lax.fori_loop(0, n_ctx, weigh, 0)

    for o in range(1, members):
        to = (g, h * members + lax.rem(m + o, members))
        send(stats, shared.at[m], ss.at[8], rs.at[5], to)
    pltpu.make_async_copy(stats, shared.at[m], rs.at[5]).start()
    gq_t[...] = jnp.zeros_like(gq_t)
    await_bytes(dl_got, rs.at[4])
    for i in range(own):
        delta[i : i + 1] = jnp.concatenate([dl_got[i * per + e] for e in range(per)], axis=1)
    forward(do_got, 3, 1)
    await_bytes(shared, rs.at[5])
    for i in range(own):
        each = [shared[e, i : i + 1] for e in range(members)]
        top = functools.reduce(jnp.maximum, each)
        mass = sum(shared[e, 4 + i : 5 + i] * jnp.exp2(each[e] - top) for e in range(members))
        lse[i : i + 1] = top + jnp.log2(mass)

    @pl.when(core == 0)
    def _():
        await_bytes(do_got, rs.at[3])

    def probs(c, i):
        return weights[c, i] * jnp.exp2(tops[c, pl.ds(i, 1)] - lse[pl.ds(i, 1)])

    def send_back(n, s, off, c, packed, back):
        place = back.at[g, pl.ds(0, cap)]

        @pl.when(s < n_ctx - 1)
        def _():
            send(packed.at[c], place, ss.at[9 + n], rs_line.at[2 + n, off], (c, d))

        @pl.when(s == n_ctx - 1)
        def _():
            pltpu.make_async_copy(packed.at[c], place, rs_line.at[2 + n, off]).start()

    zero = jnp.zeros((cap * quarter, LANES), jnp.float32)
    shape = (cap, quarter, LANES)

    def value_grads(s, _):
        off = far_first(s, n_ctx)
        c = lax.rem(g + off, n_ctx)

        acc = zero
        for i in range(own):
            cot = do_got[pl.ds(i * per, per)].reshape(rows, LANES)
            acc = acc + nn(probs(c, i).astype(jnp.bfloat16), cot)
        gv_send[c] = acc.astype(gv_send.dtype).reshape(shape)
        send_back(1, s, off, c, gv_send, v_back)
        return 0

    lax.fori_loop(0, n_ctx, value_grads, 0)

    for c in range(n_ctx):
        k_back[c, cap] = jnp.zeros(k_back.shape[2:], k_back.dtype)
        v_back[c, cap] = jnp.zeros(v_back.shape[2:], v_back.dtype)

    def finish(n, packed, back, total, out):
        for off in range(n_ctx):
            await_bytes(packed.at[0], rs_line.at[2 + n, off])

        def one(o, _):
            p = lax.rem(d + o, n_head)
            for e in range(per_dev):
                l = per_dev * p + e
                acc = back[0, jnp.clip(inv[0, l], 0, cap)].astype(jnp.float32)
                for c in range(1, n_ctx):
                    acc = acc + back[c, jnp.clip(inv[c, l], 0, cap)].astype(jnp.float32)
                total[l] = acc.astype(total.dtype)
            src = total.at[pl.ds(per_dev * p, per_dev)]
            place = out.at[h, :, 0, pl.ds(m * quarter, quarter), :]

            @pl.when(o < n_head)
            def _():
                send(src, place, ss.at[12 + n], rs.at[8 + n], (g, p))

            @pl.when(o == n_head)
            def _():
                pltpu.make_async_copy(src, place, rs.at[8 + n]).start()

            return 0

        lax.fori_loop(1, n_head + 1, one, 0)

    def key_grads(s, _):
        off = far_first(s, n_ctx)
        c = lax.rem(g + off, n_ctx)
        await_bytes(v_got.at[c], rs_line.at[1, lax.rem(n_ctx - off, n_ctx)])
        key_t = k_got[c].reshape(cap * quarter, LANES).T
        value = v_got[c].reshape(cap * quarter, LANES)

        @pl.when(s == HOOK_SUM)
        def _():
            finish(1, gv_send, v_back, v_sum, gv_out)

        acc = zero
        for i in range(own):
            query = q_got[pl.ds(i * per, per)].reshape(rows, LANES)
            cot = do_got[pl.ds(i * per, per)].reshape(rows, LANES)
            dscore = (probs(c, i) * (nt(value, cot) - delta[pl.ds(i, 1)])).astype(jnp.bfloat16)
            gq_t[i] += nn(key_t, dscore)
            acc = acc + nn(dscore, query)
        gk_send[c] = (acc * scaling).astype(gk_send.dtype).reshape(shape)
        send_back(0, s, off, c, gk_send, k_back)
        return 0

    lax.fori_loop(0, n_ctx, key_grads, 0)

    def theirs(e, _):
        i = (own // 2) * (1 - core) + e
        part = (gq_t[i].T * scaling).astype(gq_send.dtype)
        gq_send[pl.ds(i * per, per)] = part.reshape(per, LANES, LANES)
        return 0

    lax.fori_loop(0, own // 2, theirs, 0)
    send(
        gq_send.at[pl.ds(half * (1 - core), half)], gq_pair, ss.at[11], rs.at[6], (g, partner)
    )

    await_bytes(gq_pair, rs.at[6])

    def ours(e, _):
        i = (own // 2) * core + e
        part = (gq_t[i].T * scaling).reshape(per, LANES, LANES)
        part = part + gq_pair[pl.ds(e * per, per)].astype(jnp.float32)
        gq_send[pl.ds(i * per, per)] = part.astype(gq_send.dtype)
        return 0

    lax.fori_loop(0, own // 2, ours, 0)

    def send_gq(o, _):
        p = half * core + lax.rem(d + o, half)

        @pl.when(p != d)
        def _():
            send(gq_send.at[p], gq_got.at[chip], ss.at[14], rs.at[7], (g, p))

        @pl.when(p == d)
        def _():
            pltpu.make_async_copy(gq_send.at[p], gq_got.at[chip], rs.at[7]).start()

        return 0

    lax.fori_loop(0, half, send_gq, 0)

    finish(0, gk_send, k_back, k_sum, gk_out)

    await_bytes(gq_got, rs.at[7])
    pair = members // 2

    def add_q(e, _):
        acc = gq_got[pair * e].astype(jnp.float32)
        for o in range(1, pair):
            acc = acc + gq_got[pair * e + o].astype(jnp.float32)
        gq_out[e] = acc.astype(gq_out.dtype)
        return 0

    lax.fori_loop(0, n_head // members, add_q, 0)
    await_bytes(k_sum, rs.at[8])
    await_bytes(v_sum, rs.at[9])
    rows_left(do_got, 3, 1)
    await_bytes(q_got, ss.at[4])
    await_bytes(dl_got.at[pl.ds(0, n_head - 1)], ss.at[5])
    for n, ref in ((6, k_send), (7, v_send), (9, gk_send), (10, gv_send)):
        await_bytes(ref.at[pl.ds(0, n_ctx - 1)], ss.at[n])
    await_bytes(shared.at[pl.ds(0, members - 1)], ss.at[8])
    await_bytes(gq_pair, ss.at[11])
    for n, ref in ((12, k_sum), (13, v_sum)):
        await_bytes(ref.at[pl.ds(0, per_dev * (n_head - 1))], ss.at[n])
    await_bytes(gq_send.at[pl.ds(0, half - 1)], ss.at[14])

    @pl.when(d // half != core)
    def _():
        await_bytes(gq_send.at[0], ss.at[14])


def body(queries, keys, values, outputs, grad_out, block_ids, block_counts):
    f32, bf16, i32 = jnp.float32, jnp.bfloat16, jnp.int32
    n_ctx = lax.axis_size("ctx")
    n_head = lax.axis_size("head")
    kv, per_dev, _, blk, dh = keys.shape
    tokens, heads, _ = queries.shape
    members = n_head // kv
    quarter = blk // members
    group = heads // kv
    per_group = per_dev * n_head
    blocks, _, slots = block_ids.shape
    own = blocks // n_ctx
    cap = (slots + own + n_ctx - 2) // n_ctx
    part = tokens * group
    rows = blk * group
    any_ = whole(pl.ANY)
    vm = whole(VMEM)
    sm = whole(SMEM)
    limit = 60 * 2**20

    def by_kv(x):
        return jnp.transpose(x.reshape(tokens, kv, group, dh), (1, 0, 2, 3)).reshape(kv, part, dh)

    q8 = by_kv(queries)
    do8 = by_kv(grad_out)

    o8 = by_kv(outputs)
    packed = (n_ctx, cap, quarter, dh)
    back = (n_ctx, cap + 1, quarter, dh)
    held = (per_group, quarter, dh)
    spread = (n_head, part, dh)
    halves = (n_head // 2, part, dh)
    gq8, grad_keys, grad_values = pl.pallas_call(
        functools.partial(
            main_kernel, (n_ctx, n_head, members, per_dev, quarter, cap, own, rows)
        ),
        out_shape=[
            jax.ShapeDtypeStruct((kv, part, dh), bf16),
            jax.ShapeDtypeStruct(keys.shape, bf16),
            jax.ShapeDtypeStruct(keys.shape, bf16),
        ],
        in_specs=[vm] * 5 + [any_] * 2,
        out_specs=[vm, any_, any_],
        scratch_shapes=[
            VMEM((3, 8, LANES), i32),
            SMEM((8, LANES), i32),
            SMEM((8, LANES), i32),
            SMEM((8, LANES), i32),
            VMEM((kv, 1, part), f32),
            VMEM(held, bf16),
            VMEM(held, bf16),
            VMEM(packed, bf16),
            VMEM(packed, bf16),
            VMEM(packed, bf16),
            VMEM(packed, bf16),
            VMEM(spread, bf16),
            VMEM(spread, bf16),
            VMEM((n_head, 1, part), f32),
            VMEM((n_ctx, own, cap * quarter, rows), f32),
            VMEM((n_ctx, own, rows), f32),
            VMEM((8, rows), f32),
            VMEM((members, 8, rows), f32),
            VMEM((own, rows), f32),
            VMEM((own, rows), f32),
            VMEM((own, dh, rows), f32),
            VMEM(spread, bf16),
            VMEM(halves, bf16),
            VMEM(halves, bf16),
            VMEM(packed, bf16),
            VMEM(packed, bf16),
            VMEM(back, bf16),
            VMEM(back, bf16),
            VMEM(held, bf16),
            VMEM(held, bf16),
            pltpu.SemaphoreType.DMA((15,)),
            pltpu.SemaphoreType.DMA((10,)),
            pltpu.SemaphoreType.DMA((4, n_ctx)),
            pltpu.SemaphoreType.DMA((3,)),
        ],
        compiler_params=pltpu.CompilerParams(
            collective_id=0, has_side_effects=True, vmem_limit_bytes=limit
        ),
        name="main",
    )(block_ids, block_counts.T, q8, do8, o8, keys, values)
    grad_queries = jnp.transpose(gq8.reshape(kv, tokens, group, dh), (1, 0, 2, 3)).reshape(
        tokens, heads, dh
    )
    return grad_queries, grad_keys, grad_values


def solution(mesh):
    tok = P(("ctx", "head"), None, None)
    cached = P(None, "head", "ctx", None, None)
    return jax.shard_map(
        body,
        mesh=mesh,
        in_specs=(tok, cached, cached, tok, tok, P(), P()),
        out_specs=(tok, cached, cached),
        check_vma=False,
    )
```

time: 121 us -> 95.3 us (0.79)
  Pallas kernels: 112 us -> 88 us
  other arithmetic: 1.28 us -> 0 us
    pallas_call x1, Pallas kernels: 109 us -> 88 us  [body(): pl.pallas_call(functools.partial(main_kernel, (n_ctx, n_head, members, pe...]
    pallas_call x1 -> x0, Pallas kernels: 2.7 us -> none  [body(): pl.pallas_call(functools.partial(plan_kernel, (n_ctx, members, per_group,...]
    reshape x1 -> x2, local copies, waits for them, and re-layouts: 0.92 us -> 2.68 us  [by_kv(): jnp.transpose(x.reshape(tokens, kv, group, dh), (1, 0, 2, 3))]
    reduce_sum x1 -> x0, other arithmetic: 1.28 us -> none  [body(): delta = jnp.sum(grad_out.astype(f32) * outputs.astype(f32), axis=2)]
    unnamed x13 -> x10, local copies, waits for them, and re-layouts: 2.73 us -> 2.04 us
where the time goes in v3:
time: 95.3 us; the launch traced here: 95.1 us
  Pallas kernels  88 us (92%)
  local copies, waits for them, and re-layouts  6.49 us (7%)
    pallas_call x1, Pallas kernels, body(): pl.pallas_call(functools.partial(main_kernel, (n_ctx, n_head, members, pe...  88 us
    reshape x2, local copies, waits for them, and re-layouts, by_kv(): jnp.transpose(x.reshape(tokens, kv, group, dh), (1, 0, 2, 3))  2.68 us
    unnamed x10, local copies, waits for them, and re-layouts  2.04 us

profile of v3, /device:TPU:1, one launch (start us, length us, event | category | flops | bytes accessed | tf_op | source)
XLA Modules:
  0.0 95.1 jit_solution(9257430903338455571)
XLA Ops:
  0.6 0.0 copy-start
  0.6 0.0 copy-start.3
  0.7 1.8 %copy_bitcast_fusion.3.q = bf16[8,128,128]{2,1,0:T(8,128)(2,1)} fusion(bf16[16,64,128]{2,1,0:T(8,128)(2,1)} %param.7), kind=kLoop, calls=%fused_computation.3 | loop fusion | bytes 524288 | tf_op jit(solution)/shard_map/reshape | solution.py:546
  2.4 0.0 copy-done
  2.4 0.0 copy-done.3
  2.4 0.9 copy_bitcast_fusion.1
  3.3 88.0 %main.1 = (bf16[8,128,128]{2,1,0:T(8,128)(2,1)}, bf16[8,2,1,128,128]{4,3,2,1,0:T(8,128)(2,1)}, bf16[8,2,1,128,128]{4,3,2,1,0:T(8,128)(2,1)}) custom-call(s32[32,8,48]{2,1,0:T(8,128)} %lists.1, s32[8,32]{1,0:T(8,128)} %bitcast.29, bf16[8,128,128]{2,1,0:T(8,128)(2,1)} %copy_bitcast_fusion.3.q, bf16[8,128,128]{2,1,0:T(8,128)(2,1)} %get-tuple-element.10.do, ...), custom_call_target="tpu_custom_call" | custom-call | tf_op jit(solution)/shard_map/main/pallas_call | solution.py:557
  91.3 0.0 copy-start.2
  91.3 1.8 %copy_bitcast_fusion = bf16[16,64,128]{2,1,0:T(8,128)(2,1)} fusion(bf16[8,128,128]{2,1,0:T(8,128)(2,1)} %get-tuple-element.6), kind=kLoop, calls=%fused_computation | loop fusion | bytes 524288 | tf_op jit(solution)/shard_map/reshape | solution.py:609
  93.1 0.0 copy-done.2
  93.1 0.0 copy-start.1
  93.1 0.8 copy.20
  93.9 0.4 copy-done.1
  94.3 0.8 copy.21
Async XLA Ops:
  0.6 1.8 %copy-start = (bf16[16,64,128]{2,1,0:T(8,128)(2,1)S(1)}, bf16[16,64,128]{2,1,0:T(8,128)(2,1)}, u32[]{:S(2)}) copy-start(bf16[16,64,128]{2,1,0:T(8,128)(2,1)} %param.11) | copy-start | bytes 786436
  0.6 1.8 %copy-start.3 = (bf16[16,64,128]{2,1,0:T(8,128)(2,1)S(1)}, bf16[16,64,128]{2,1,0:T(8,128)(2,1)}, u32[]{:S(2)}) copy-start(bf16[16,64,128]{2,1,0:T(8,128)(2,1)} %param.10) | copy-start | bytes 786436
  91.3 1.8 %copy-start.2 = (bf16[8,2,1,128,128]{4,3,2,1,0:T(8,128)(2,1)S(1)}, bf16[8,2,1,128,128]{4,3,2,1,0:T(8,128)(2,1)}, u32[]{:S(2)}) copy-start(bf16[8,2,1,128,128]{4,3,2,1,0:T(8,128)(2,1)} %get-tuple-element.15) | copy-start | bytes 1572868
  93.1 1.2 %copy-start.1 = (bf16[8,2,1,128,128]{4,3,2,1,0:T(8,128)(2,1)S(1)}, bf16[8,2,1,128,128]{4,3,2,1,0:T(8,128)(2,1)}, u32[]{:S(2)}) copy-start(bf16[8,2,1,128,128]{4,3,2,1,0:T(8,128)(2,1)} %get-tuple-element.16) | copy-start | bytes 1572868

commit v4 on v3

--- a/solution.py
+++ b/solution.py
@@ -14,8 +14,9 @@
 LOG2E = 1.4426950408889634
 LANES = 128
 FAR = 4096
-HOOK = 2
-HOOK_SUM = 6
+HOOK = 4
+HOOK_SUM = 3
+HOOK_GQ = 1
 
 
 def whole(space):
@@ -177,8 +178,11 @@
     shared,
     lse,
     delta,
-    gq_t,
+    keys_t,
+    ds_held,
     gq_send,
+    gq_full,
+    gk_acc,
     gq_pair,
     gq_got,
     gk_send,
@@ -190,6 +194,7 @@
     ss,
     rs,
     rs_line,
+    rs_q,
     local_sem,
 ):
     n_ctx, n_head, members, per_dev, quarter, cap, own, rows = dims
@@ -234,21 +239,21 @@
     def held_left(n, held):
         await_bytes(held.at[pl.ds(0, per_dev * (n_head - 1))], ss.at[n])
 
-    def send_rows(src, got, n, to_core):
+    def send_rows(src, got, n, r_sem, to_core):
         def one(o, _):
             t = lax.rem(chip + o, chips)
-            send(src.at[2 * t // members], got.at[d], ss.at[n], rs.at[n], (g, 2 * t + to_core))
+            send(src.at[2 * t // members], got.at[d], ss.at[n], r_sem, (g, 2 * t + to_core))
             return 0
 
         lax.fori_loop(1, chips, one, 0)
 
         @pl.when(core == to_core)
         def _():
-            pltpu.make_async_copy(src.at[h], got.at[d], rs.at[n]).start()
+            pltpu.make_async_copy(src.at[h], got.at[d], r_sem).start()
 
         @pl.when(core != to_core)
         def _():
-            send(src.at[h], got.at[d], ss.at[n], rs.at[n], (g, partner))
+            send(src.at[h], got.at[d], ss.at[n], r_sem, (g, partner))
 
     def rows_left(got, n, to_core):
         await_bytes(got.at[pl.ds(0, chips - 1)], ss.at[n])
@@ -289,34 +294,36 @@
     plan((n_ctx, members, per_dev * n_head, own, cap), lists, counts, *[plans.at[e] for e in range(3)])
     for e, place in enumerate((ids, thr, inv)):
         pltpu.make_async_copy(plans.at[e], place, local_sem.at[e]).start()
+    for e, place in enumerate((ids, thr, inv)):
+        pltpu.make_async_copy(plans.at[e], place, local_sem.at[e]).wait()
+
+    held_left(0, k_held)
+    send_rows(q, q_got, 2, rs_q.at[d // per], 0)
+    send_retained(0, k_held, k_send, k_got)
     for e in range(n_head // members):
         product = do[e].astype(jnp.float32) * out8[e].astype(jnp.float32)
         dl_send[e] = jnp.sum(product.T, axis=0, keepdims=True)
-    for e, place in enumerate((ids, thr, inv)):
-        pltpu.make_async_copy(plans.at[e], place, local_sem.at[e]).wait()
-
-    held_left(0, k_held)
-    send_rows(q, q_got, 2, 0)
-    send_retained(0, k_held, k_send, k_got)
+
+    def send_delta(o, _):
+        p = lax.rem(d + o, n_head)
+        send(dl_send.at[p // members], dl_got.at[d], ss.at[5], rs.at[4], (g, p))
+        return 0
+
+    lax.fori_loop(1, n_head, send_delta, 0)
+    pltpu.make_async_copy(dl_send.at[h], dl_got.at[d], rs.at[4]).start()
     rows_left(q_got, 2, 0)
     send_held(1, vals, v_held)
-    forward(q_got, 2, 0)
-
-    @pl.when(core == 1)
+
+    @pl.when(core == 0)
     def _():
-        await_bytes(q_got, rs.at[2])
+        for i in range(own):
+            block = q_got.at[pl.ds(i * per, per)]
+            await_bytes(block, rs_q.at[i])
+            send(block, block, ss.at[4], rs_q.at[i], (g, partner))
+
+    send_rows(do, do_got, 3, rs.at[3], 1)
 
     def more():
-        held_left(1, v_held)
-        send_rows(do, do_got, 3, 1)
-
-        def send_delta(o, _):
-            p = lax.rem(d + o, n_head)
-            send(dl_send.at[p // members], dl_got.at[d], ss.at[5], rs.at[4], (g, p))
-            return 0
-
-        lax.fori_loop(1, n_head, send_delta, 0)
-        pltpu.make_async_copy(dl_send.at[h], dl_got.at[d], rs.at[4]).start()
         send_retained(1, v_held, v_send, v_got)
 
     gap = reach(rows, quarter, m)
@@ -332,6 +339,11 @@
             more()
 
         for i in range(own):
+
+            @pl.when((s == 0) & (core == 1))
+            def _(i=i):
+                await_bytes(q_got.at[pl.ds(i * per, per)], rs_q.at[i])
+
             key = k_got[c].reshape(cap * quarter, LANES)
             query = q_got[pl.ds(i * per, per)].reshape(rows, LANES)
             score = scaled(thr, i, c, n_ctx, cap, quarter, gap, nt(key, query))
@@ -352,7 +364,7 @@
         to = (g, h * members + lax.rem(m + o, members))
         send(stats, shared.at[m], ss.at[8], rs.at[5], to)
     pltpu.make_async_copy(stats, shared.at[m], rs.at[5]).start()
-    gq_t[...] = jnp.zeros_like(gq_t)
+    keys_t[...] = k_got[...].reshape(n_ctx * cap * quarter, LANES).T
     await_bytes(dl_got, rs.at[4])
     for i in range(own):
         delta[i : i + 1] = jnp.concatenate([dl_got[i * per + e] for e in range(per)], axis=1)
@@ -430,67 +442,74 @@
 
         lax.fori_loop(1, n_head + 1, one, 0)
 
-    def key_grads(s, _):
-        off = far_first(s, n_ctx)
-        c = lax.rem(g + off, n_ctx)
-        await_bytes(v_got.at[c], rs_line.at[1, lax.rem(n_ctx - off, n_ctx)])
-        key_t = k_got[c].reshape(cap * quarter, LANES).T
+    few = per // 2
+    both = own // 2
+
+    def exchange(side):
+        for i in range(both * side, both * side + both):
+            ds_all = ds_held[i - both * side].reshape(n_ctx * cap * quarter, rows)
+            gq_full[i] = (nn(keys_t[...], ds_all).T * scaling).reshape(per, LANES, LANES)
+            theirs = pl.ds(few * (1 - core), few)
+            place = gq_send.at[pl.ds(i * per + few * (1 - core), few)]
+            place[...] = gq_full[i, theirs].astype(gq_send.dtype)
+            send(place, gq_pair.at[i], ss.at[11], rs.at[6 + 4 * side], (g, partner))
+
+    def combine(side):
+        await_bytes(gq_pair.at[pl.ds(both * side, both)], rs.at[6 + 4 * side])
+        for i in range(both * side, both * side + both):
+            part = gq_full[i, pl.ds(few * core, few)] + gq_pair[i].astype(jnp.float32)
+            gq_send[pl.ds(i * per + few * core, few)] = part.astype(gq_send.dtype)
+            for j in range(few):
+                p = i * per + few * core + j
+
+                @pl.when(p != d)
+                def _(p=p):
+                    send(gq_send.at[p], gq_got.at[chip], ss.at[14], rs.at[7], (g, p))
+
+                @pl.when(p == d)
+                def _(p=p):
+                    pltpu.make_async_copy(gq_send.at[p], gq_got.at[chip], rs.at[7]).start()
+
+    def key_part(c, side, acc):
         value = v_got[c].reshape(cap * quarter, LANES)
-
-        @pl.when(s == HOOK_SUM)
-        def _():
-            finish(1, gv_send, v_back, v_sum, gv_out)
-
-        acc = zero
-        for i in range(own):
+        for i in range(both * side, both * side + both):
             query = q_got[pl.ds(i * per, per)].reshape(rows, LANES)
             cot = do_got[pl.ds(i * per, per)].reshape(rows, LANES)
             dscore = (probs(c, i) * (nt(value, cot) - delta[pl.ds(i, 1)])).astype(jnp.bfloat16)
-            gq_t[i] += nn(key_t, dscore)
+            ds_held[i - both * side, c] = dscore
             acc = acc + nn(dscore, query)
+        return acc
+
+    def first_side(s, _):
+        off = near_first(s, n_ctx)
+        c = lax.rem(g - off + n_ctx, n_ctx)
+        await_bytes(v_got.at[c], rs_line.at[1, off])
+        gk_acc[c] = key_part(c, 0, zero)
+        return 0
+
+    lax.fori_loop(0, n_ctx, first_side, 0)
+    exchange(0)
+
+    def second_side(s, _):
+        off = far_first(s, n_ctx)
+        c = lax.rem(g + off, n_ctx)
+
+        @pl.when(s == HOOK_GQ)
+        def _():
+            combine(0)
+
+        @pl.when(s == HOOK_SUM)
+        def _():
+            finish(1, gv_send, v_back, v_sum, gv_out)
+
+        acc = key_part(c, 1, gk_acc[c])
         gk_send[c] = (acc * scaling).astype(gk_send.dtype).reshape(shape)
         send_back(0, s, off, c, gk_send, k_back)
         return 0
 
-    lax.fori_loop(0, n_ctx, key_grads, 0)
-
-    def theirs(e, _):
-        i = (own // 2) * (1 - core) + e
-        part = (gq_t[i].T * scaling).astype(gq_send.dtype)
-        gq_send[pl.ds(i * per, per)] = part.reshape(per, LANES, LANES)
-        return 0
-
-    lax.fori_loop(0, own // 2, theirs, 0)
-    send(
-        gq_send.at[pl.ds(half * (1 - core), half)], gq_pair, ss.at[11], rs.at[6], (g, partner)
-    )
-
-    await_bytes(gq_pair, rs.at[6])
-
-    def ours(e, _):
-        i = (own // 2) * core + e
-        part = (gq_t[i].T * scaling).reshape(per, LANES, LANES)
-        part = part + gq_pair[pl.ds(e * per, per)].astype(jnp.float32)
-        gq_send[pl.ds(i * per, per)] = part.astype(gq_send.dtype)
-        return 0
-
-    lax.fori_loop(0, own // 2, ours, 0)
-
-    def send_gq(o, _):
-        p = half * core + lax.rem(d + o, half)
-
-        @pl.when(p != d)
-        def _():
-            send(gq_send.at[p], gq_got.at[chip], ss.at[14], rs.at[7], (g, p))
-
-        @pl.when(p == d)
-        def _():
-            pltpu.make_async_copy(gq_send.at[p], gq_got.at[chip], rs.at[7]).start()
-
-        return 0
-
-    lax.fori_loop(0, half, send_gq, 0)
-
+    lax.fori_loop(0, n_ctx, second_side, 0)
+    exchange(1)
+    combine(1)
     finish(0, gk_send, k_back, k_sum, gk_out)
 
     await_bytes(gq_got, rs.at[7])
@@ -506,6 +525,7 @@
     lax.fori_loop(0, n_head // members, add_q, 0)
     await_bytes(k_sum, rs.at[8])
     await_bytes(v_sum, rs.at[9])
+    held_left(1, v_held)
     rows_left(do_got, 3, 1)
     await_bytes(q_got, ss.at[4])
     await_bytes(dl_got.at[pl.ds(0, n_head - 1)], ss.at[5])
@@ -517,7 +537,7 @@
         await_bytes(ref.at[pl.ds(0, per_dev * (n_head - 1))], ss.at[n])
     await_bytes(gq_send.at[pl.ds(0, half - 1)], ss.at[14])
 
-    @pl.when(d // half != core)
+    @pl.when((d % per) // few != core)
     def _():
         await_bytes(gq_send.at[0], ss.at[14])
 
@@ -586,9 +606,12 @@
             VMEM((members, 8, rows), f32),
             VMEM((own, rows), f32),
             VMEM((own, rows), f32),
-            VMEM((own, dh, rows), f32),
+            VMEM((dh, n_ctx * cap * quarter), bf16),
+            VMEM((own // 2, n_ctx, cap * quarter, rows), bf16),
             VMEM(spread, bf16),
-            VMEM(halves, bf16),
+            VMEM((own, rows // LANES, LANES, dh), f32),
+            VMEM((n_ctx, cap * quarter, dh), f32),
+            VMEM((own, rows // LANES // 2, LANES, dh), bf16),
             VMEM(halves, bf16),
             VMEM(packed, bf16),
             VMEM(packed, bf16),
@@ -597,8 +620,9 @@
             VMEM(held, bf16),
             VMEM(held, bf16),
             pltpu.SemaphoreType.DMA((15,)),
-            pltpu.SemaphoreType.DMA((10,)),
+            pltpu.SemaphoreType.DMA((11,)),
             pltpu.SemaphoreType.DMA((4, n_ctx)),
+            pltpu.SemaphoreType.DMA((own,)),
             pltpu.SemaphoreType.DMA((3,)),
         ],
         compiler_params=pltpu.CompilerParams(

time: 95.3 us -> 92.2 us (0.967)
  Pallas kernels: 88 us -> 84.2 us
    pallas_call x1, Pallas kernels: 88 us -> 84.2 us  [body(): pl.pallas_call(functools.partial(main_kernel, (n_ctx, n_head, members, pe...]
where the time goes in v4:
time: 92.2 us; the launch traced here: 91.4 us
  Pallas kernels  84.2 us (91%)
  local copies, waits for them, and re-layouts  6.49 us (7%)
    pallas_call x1, Pallas kernels, body(): pl.pallas_call(functools.partial(main_kernel, (n_ctx, n_head, members, pe...  84.2 us
    reshape x2, local copies, waits for them, and re-layouts, by_kv(): jnp.transpose(x.reshape(tokens, kv, group, dh), (1, 0, 2, 3))  2.68 us
    unnamed x10, local copies, waits for them, and re-layouts  2.04 us

profile of v4, /device:TPU:1, one launch (start us, length us, event | category | flops | bytes accessed | tf_op | source)
XLA Modules:
  0.0 91.4 jit_solution(13534499570798329230)
XLA Ops:
  0.6 0.0 copy-start
  0.6 0.0 copy-start.3
  0.7 1.8 %copy_bitcast_fusion.3.q = bf16[8,128,128]{2,1,0:T(8,128)(2,1)} fusion(bf16[16,64,128]{2,1,0:T(8,128)(2,1)} %param.7), kind=kLoop, calls=%fused_computation.3 | loop fusion | bytes 524288 | tf_op jit(solution)/shard_map/reshape | solution.py:566
  2.4 0.0 copy-done
  2.4 0.0 copy-done.3
  2.4 0.9 %copy_bitcast_fusion.1 = (bf16[8,128,128]{2,1,0:T(8,128)(2,1)}, bf16[8,128,128]{2,1,0:T(8,128)(2,1)}) fusion(bf16[16,64,128]{2,1,0:T(8,128)(2,1)S(1)} %copy-done, bf16[16,64,128]{2,1,0:T(8,128)(2,1)S(1)} %copy-done.3), kind=kLoop, calls=%fused_computation.1 | loop fusion | bytes 1048576 | tf_op jit(solution)/shard_map/reshape | solution.py:566
  3.3 84.2 %main.1 = (bf16[8,128,128]{2,1,0:T(8,128)(2,1)}, bf16[8,2,1,128,128]{4,3,2,1,0:T(8,128)(2,1)}, bf16[8,2,1,128,128]{4,3,2,1,0:T(8,128)(2,1)}) custom-call(s32[32,8,48]{2,1,0:T(8,128)} %lists.1, s32[8,32]{1,0:T(8,128)} %bitcast.29, bf16[8,128,128]{2,1,0:T(8,128)(2,1)} %copy_bitcast_fusion.3.q, bf16[8,128,128]{2,1,0:T(8,128)(2,1)} %get-tuple-element.10.do, ...), custom_call_target="tpu_custom_call" | custom-call | tf_op jit(solution)/shard_map/main/pallas_call | solution.py:577
  87.6 0.0 copy-start.2
  87.6 1.8 %copy_bitcast_fusion = bf16[16,64,128]{2,1,0:T(8,128)(2,1)} fusion(bf16[8,128,128]{2,1,0:T(8,128)(2,1)} %get-tuple-element.6), kind=kLoop, calls=%fused_computation | loop fusion | bytes 524288 | tf_op jit(solution)/shard_map/reshape | solution.py:633
  89.3 0.0 copy-done.2
  89.3 0.0 copy-start.1
  89.3 0.8 copy.20
  90.1 0.4 copy-done.1
  90.6 0.8 copy.21
Async XLA Ops:
  0.6 1.8 %copy-start = (bf16[16,64,128]{2,1,0:T(8,128)(2,1)S(1)}, bf16[16,64,128]{2,1,0:T(8,128)(2,1)}, u32[]{:S(2)}) copy-start(bf16[16,64,128]{2,1,0:T(8,128)(2,1)} %param.11) | copy-start | bytes 786436
  0.6 1.8 %copy-start.3 = (bf16[16,64,128]{2,1,0:T(8,128)(2,1)S(1)}, bf16[16,64,128]{2,1,0:T(8,128)(2,1)}, u32[]{:S(2)}) copy-start(bf16[16,64,128]{2,1,0:T(8,128)(2,1)} %param.10) | copy-start | bytes 786436
  87.6 1.8 %copy-start.2 = (bf16[8,2,1,128,128]{4,3,2,1,0:T(8,128)(2,1)S(1)}, bf16[8,2,1,128,128]{4,3,2,1,0:T(8,128)(2,1)}, u32[]{:S(2)}) copy-start(bf16[8,2,1,128,128]{4,3,2,1,0:T(8,128)(2,1)} %get-tuple-element.15) | copy-start | bytes 1572868
  89.3 1.2 %copy-start.1 = (bf16[8,2,1,128,128]{4,3,2,1,0:T(8,128)(2,1)S(1)}, bf16[8,2,1,128,128]{4,3,2,1,0:T(8,128)(2,1)}, u32[]{:S(2)}) copy-start(bf16[8,2,1,128,128]{4,3,2,1,0:T(8,128)(2,1)} %get-tuple-element.16) | copy-start | bytes 1572868

commit v5 on v4

--- a/solution.py
+++ b/solution.py
@@ -14,7 +14,7 @@
 LOG2E = 1.4426950408889634
 LANES = 128
 FAR = 4096
-HOOK = 4
+HOOK = 5
 HOOK_SUM = 3
 HOOK_GQ = 1
 

time: 92.2 us -> 92.8 us (level)
  no operation moved by 1% of the time
where the time goes in v5:
time: 92.8 us; the launch traced here: 91.5 us
  Pallas kernels  84.3 us (91%)
  local copies, waits for them, and re-layouts  6.49 us (7%)
    pallas_call x1, Pallas kernels, body(): pl.pallas_call(functools.partial(main_kernel, (n_ctx, n_head, members, pe...  84.3 us
    reshape x2, local copies, waits for them, and re-layouts, by_kv(): jnp.transpose(x.reshape(tokens, kv, group, dh), (1, 0, 2, 3))  2.68 us
    unnamed x10, local copies, waits for them, and re-layouts  2.04 us

profile of v5, /device:TPU:1, one launch (start us, length us, event | category | flops | bytes accessed | tf_op | source)
XLA Modules:
  0.0 91.5 jit_solution(9145964647568920078)
XLA Ops:
  0.6 0.0 copy-start
  0.6 0.0 copy-start.3
  0.7 1.8 %copy_bitcast_fusion.3.q = bf16[8,128,128]{2,1,0:T(8,128)(2,1)} fusion(bf16[16,64,128]{2,1,0:T(8,128)(2,1)} %param.7), kind=kLoop, calls=%fused_computation.3 | loop fusion | bytes 524288 | tf_op jit(solution)/shard_map/reshape | solution.py:566
  2.4 0.0 copy-done
  2.4 0.0 copy-done.3
  2.4 0.9 %copy_bitcast_fusion.1 = (bf16[8,128,128]{2,1,0:T(8,128)(2,1)}, bf16[8,128,128]{2,1,0:T(8,128)(2,1)}) fusion(bf16[16,64,128]{2,1,0:T(8,128)(2,1)S(1)} %copy-done, bf16[16,64,128]{2,1,0:T(8,128)(2,1)S(1)} %copy-done.3), kind=kLoop, calls=%fused_computation.1 | loop fusion | bytes 1048576 | tf_op jit(solution)/shard_map/reshape | solution.py:566
  3.3 84.3 %main.1 = (bf16[8,128,128]{2,1,0:T(8,128)(2,1)}, bf16[8,2,1,128,128]{4,3,2,1,0:T(8,128)(2,1)}, bf16[8,2,1,128,128]{4,3,2,1,0:T(8,128)(2,1)}) custom-call(s32[32,8,48]{2,1,0:T(8,128)} %lists.1, s32[8,32]{1,0:T(8,128)} %bitcast.29, bf16[8,128,128]{2,1,0:T(8,128)(2,1)} %copy_bitcast_fusion.3.q, bf16[8,128,128]{2,1,0:T(8,128)(2,1)} %get-tuple-element.10.do, ...), custom_call_target="tpu_custom_call" | custom-call | tf_op jit(solution)/shard_map/main/pallas_call | solution.py:577
  87.7 0.0 copy-start.2
  87.7 1.8 %copy_bitcast_fusion = bf16[16,64,128]{2,1,0:T(8,128)(2,1)} fusion(bf16[8,128,128]{2,1,0:T(8,128)(2,1)} %get-tuple-element.6), kind=kLoop, calls=%fused_computation | loop fusion | bytes 524288 | tf_op jit(solution)/shard_map/reshape | solution.py:633
  89.5 0.0 copy-done.2
  89.5 0.0 copy-start.1
  89.5 0.8 copy.20
  90.3 0.4 copy-done.1
  90.7 0.8 copy.21
Async XLA Ops:
  0.6 1.8 %copy-start = (bf16[16,64,128]{2,1,0:T(8,128)(2,1)S(1)}, bf16[16,64,128]{2,1,0:T(8,128)(2,1)}, u32[]{:S(2)}) copy-start(bf16[16,64,128]{2,1,0:T(8,128)(2,1)} %param.11) | copy-start | bytes 786436
  0.6 1.8 %copy-start.3 = (bf16[16,64,128]{2,1,0:T(8,128)(2,1)S(1)}, bf16[16,64,128]{2,1,0:T(8,128)(2,1)}, u32[]{:S(2)}) copy-start(bf16[16,64,128]{2,1,0:T(8,128)(2,1)} %param.10) | copy-start | bytes 786436
  87.7 1.8 %copy-start.2 = (bf16[8,2,1,128,128]{4,3,2,1,0:T(8,128)(2,1)S(1)}, bf16[8,2,1,128,128]{4,3,2,1,0:T(8,128)(2,1)}, u32[]{:S(2)}) copy-start(bf16[8,2,1,128,128]{4,3,2,1,0:T(8,128)(2,1)} %get-tuple-element.15) | copy-start | bytes 1572868
  89.5 1.2 %copy-start.1 = (bf16[8,2,1,128,128]{4,3,2,1,0:T(8,128)(2,1)S(1)}, bf16[8,2,1,128,128]{4,3,2,1,0:T(8,128)(2,1)}, u32[]{:S(2)}) copy-start(bf16[8,2,1,128,128]{4,3,2,1,0:T(8,128)(2,1)} %get-tuple-element.16) | copy-start | bytes 1572868
